TPU v7x, 256 devices: a whole 4x4x8 slice. The times are simulated.
256 devices in a mesh: trk: 32 (over x, y, z_hi), frm: 8 (over z_lo, core).
Axes of the slice: x: 4, y: 4, z: 8 (z_hi: 2, z_lo: 4; z = z_hi * 4 + z_lo), core: 2. Of those that a mesh axis runs over, the one named last changes fastest.
Arguments:
- tokens: bfloat16 [2048, 128, 384], P('trk', 'frm'), may hold values from -6 to 6
- visible: int32 [2048, 128], P('trk', 'frm'), may hold values 0 or 1
- virtual: bfloat16 [128, 64, 384], P('frm'), may hold values from -6 to 6
- gains: float32 [7, 384], replicated, may hold values from 0.1 to 1.9
- w_time_qkv: bfloat16 [384, 1152], replicated, may hold values from -9.3386796 to 9.3386796
- w_time_o: bfloat16 [384, 384], replicated, may hold values from -0.3125 to 0.3125
- w_read_q: bfloat16 [384, 384], replicated, may hold values from -0.30618622 to 0.30618622
- w_read_kv: bfloat16 [384, 768], replicated, may hold values from -18.473235143489802 to 18.473235143489802
- w_read_o: bfloat16 [384, 384], replicated, may hold values from -0.3125 to 0.3125
- w_write_q: bfloat16 [384, 384], replicated, may hold values from -0.3125 to 0.3125
- w_write_kv: bfloat16 [384, 768], replicated, may hold values from -0.3125 to 0.3125
- w_write_o: bfloat16 [384, 384], replicated, may hold values from -0.3125 to 0.3125
- w_up: bfloat16 [384, 1536], replicated, may hold values from -0.3125 to 0.3125
- w_down: bfloat16 [1536, 384], replicated, may hold values from -0.15625 to 0.15625
- v_up: bfloat16 [384, 1536], replicated, may hold values from -0.3125 to 0.3125
- v_down: bfloat16 [1536, 384], replicated, may hold values from -0.15625 to 0.15625
Outputs:
- track_out: bfloat16 [2048, 128, 384], P('trk', 'frm')
- virt_out: bfloat16 [128, 64, 384], P('frm')
All inputs are finite; a program needn't handle non-finite values. No bound on the sum of `visible` on one device may be relied on, other than what follows from the above.
Results may differ from a plain program's by a relative error of at most 0.025.
The roundings to bfloat16 on the way count: a program that leaves them out, or rounds other values in their place, can miss the bound.
Values may be sent and summed in bfloat16 or wider, within the bound.
A program may use at most 128 MiB of HBM per device.

v0:
```python
import math

import jax
import jax.numpy as jnp
from jax import lax
from jax.sharding import PartitionSpec as P

HEADS = 8


penalty = 4.0
epsilon = 1e-05


def layer_norm(inputs, gain_row):
    values = inputs.astype(jnp.float32)
    center = values - jnp.mean(values, axis=-1, keepdims=True)
    spread = jnp.mean(center * center, axis=-1, keepdims=True)
    return center * lax.rsqrt(spread + epsilon) * gain_row


def attend_heads(queries, keys, values, key_bias):
    batch, rows_q, model_width = queries.shape
    rows_k = keys.shape[1]
    head_size = model_width // HEADS
    qheads = queries.reshape(batch, rows_q, HEADS, head_size)
    kheads = keys.reshape(batch, rows_k, HEADS, head_size)
    vheads = values.reshape(batch, rows_k, HEADS, head_size)
    scores = jnp.einsum(
        "bqhd,bkhd->bhqk", qheads, kheads, preferred_element_type=jnp.float32
    ) / math.sqrt(head_size)
    if key_bias is not None:
        scores = scores + key_bias.astype(jnp.float32)[:, None, None, :]
    peak = jnp.max(scores, axis=-1, keepdims=True)
    expos = jnp.exp(scores - peak)
    totals = jnp.sum(expos, axis=-1)
    numer = jnp.einsum(
        "bhqk,bkhd->bqhd", expos.astype(jnp.bfloat16), vheads, preferred_element_type=jnp.float32
    )
    output = numer / jnp.transpose(totals, (0, 2, 1))[..., None]
    return output.reshape(batch, rows_q, model_width).astype(jnp.bfloat16)


def feed_forward(normed, w_first, w_second):
    middle = jax.nn.gelu(
        jnp.dot(normed, w_first, preferred_element_type=jnp.float32), approximate=True
    )
    return jnp.dot(middle.astype(jnp.bfloat16), w_second, preferred_element_type=jnp.float32)


def virtual_update(virt_rows, readout, gains, w_read_o, v_up, v_down, w_write_kv):
    virt1 = (
        virt_rows.astype(jnp.float32)
        + jnp.dot(readout, w_read_o, preferred_element_type=jnp.float32)
    ).astype(jnp.bfloat16)
    normed = layer_norm(virt1, gains[5]).astype(jnp.bfloat16)
    final = (virt1.astype(jnp.float32) + feed_forward(normed, v_up, v_down)).astype(jnp.bfloat16)
    keyed = layer_norm(final, gains[6]).astype(jnp.bfloat16)
    write_pairs = jnp.dot(keyed, w_write_kv, preferred_element_type=jnp.float32).astype(
        jnp.bfloat16
    )
    return (final, write_pairs)


def shards(
    tokens,
    visible,
    virtual,
    gains,
    w_time_qkv,
    w_time_o,
    w_read_q,
    w_read_kv,
    w_read_o,
    w_write_q,
    w_write_kv,
    w_write_o,
    w_up,
    w_down,
    v_up,
    v_down,
):
    trk_rows, frm_rows, model_width = tokens.shape
    frm_count = lax.axis_size("frm")
    per_group = trk_rows // frm_count
    visible_bias = ((visible.astype(jnp.float32) - 1.0) * penalty).astype(jnp.bfloat16)
    normed = layer_norm(tokens, gains[0]).astype(jnp.bfloat16)
    normed_part = lax.all_to_all(
        normed.reshape(frm_count, per_group, frm_rows, model_width),
        "frm",
        split_axis=0,
        concat_axis=2,
        tiled=True,
    )
    bias_part = lax.all_to_all(
        visible_bias.reshape(frm_count, per_group, frm_rows),
        "frm",
        split_axis=0,
        concat_axis=2,
        tiled=True,
    )
    triple = jnp.dot(normed_part[0], w_time_qkv, preferred_element_type=jnp.float32).astype(
        jnp.bfloat16
    )
    attended = attend_heads(
        triple[..., :model_width],
        triple[..., model_width : 2 * model_width],
        triple[..., 2 * model_width :],
        bias_part[0],
    )
    projected = jnp.dot(attended, w_time_o, preferred_element_type=jnp.float32).astype(
        jnp.bfloat16
    )[None]
    regrouped = lax.all_to_all(projected, "frm", split_axis=2, concat_axis=0, tiled=True)
    time_out = regrouped.reshape(trk_rows, frm_rows, model_width)
    first = (tokens.astype(jnp.float32) + time_out.astype(jnp.float32)).astype(jnp.bfloat16)
    normed_two = layer_norm(first, gains[1]).astype(jnp.bfloat16)
    pairs = jnp.dot(normed_two, w_read_kv, preferred_element_type=jnp.float32).astype(jnp.bfloat16)
    vnormed = layer_norm(virtual, gains[4]).astype(jnp.bfloat16)
    vquery = jnp.dot(vnormed, w_read_q, preferred_element_type=jnp.float32).astype(jnp.bfloat16)
    virt_count = virtual.shape[1]
    head_size = model_width // HEADS
    qheads = vquery.reshape(frm_rows, virt_count, HEADS, head_size)
    kheads = pairs[..., :model_width].reshape(trk_rows, frm_rows, HEADS, head_size)
    vheads = pairs[..., model_width:].reshape(trk_rows, frm_rows, HEADS, head_size)
    scores = jnp.einsum(
        "fvhd,tfhd->fhvt", qheads, kheads, preferred_element_type=jnp.float32
    ) / math.sqrt(head_size)
    scores = scores + jnp.transpose(visible_bias.astype(jnp.float32))[:, None, None, :]
    peak = lax.pmax(jnp.max(scores, axis=-1).astype(jnp.bfloat16), "trk").astype(jnp.float32)
    expos = jnp.exp(scores - peak[..., None])
    totals = jnp.transpose(jnp.sum(expos, axis=-1), (0, 2, 1))
    numer = jnp.einsum(
        "fhvt,tfhd->fvhd", expos.astype(jnp.bfloat16), vheads, preferred_element_type=jnp.float32
    )
    numer_all, totals_all = (
        lax.psum(numer.astype(jnp.bfloat16), "trk").astype(jnp.float32),
        lax.psum(totals.astype(jnp.bfloat16), "trk").astype(jnp.float32),
    )
    readout = (
        (numer_all / totals_all[..., None])
        .reshape(frm_rows, virt_count, model_width)
        .astype(jnp.bfloat16)
    )
    virt_out, write_pairs = virtual_update(
        virtual, readout, gains, w_read_o, v_up, v_down, w_write_kv
    )
    normed_three = layer_norm(first, gains[2]).astype(jnp.bfloat16)
    queries = jnp.dot(normed_three, w_write_q, preferred_element_type=jnp.float32).astype(
        jnp.bfloat16
    )
    attended = attend_heads(
        jnp.transpose(queries, (1, 0, 2)),
        write_pairs[..., :model_width],
        write_pairs[..., model_width:],
        None,
    )
    attended = jnp.transpose(attended, (1, 0, 2))
    second = (
        first.astype(jnp.float32) + jnp.dot(attended, w_write_o, preferred_element_type=jnp.float32)
    ).astype(jnp.bfloat16)
    normed_four = layer_norm(second, gains[3]).astype(jnp.bfloat16)
    track_out = (second.astype(jnp.float32) + feed_forward(normed_four, w_up, w_down)).astype(
        jnp.bfloat16
    )
    return (track_out, virt_out)


def solution(mesh):
    in_specs = (
        P("trk", "frm", None),
        P("trk", "frm"),
        P("frm", None, None),
        P(),
        P(),
        P(),
        P(),
        P(),
        P(),
        P(),
        P(),
        P(),
        P(),
        P(),
        P(),
        P(),
    )
    out_specs = (P("trk", "frm", None), P("frm", None, None))
    return jax.shard_map(shards, mesh=mesh, in_specs=in_specs, out_specs=out_specs, check_vma=False)
```

profile of v0, /device:TPU:32, one launch (start us, length us, event | category | flops | bytes accessed | tf_op | source)
XLA Modules:
  0.0 795.4 jit_solution(15829206192557470184)
XLA Ops:
  8.7 6.0 all-to-all-start.1
  20.5 5.1 all-to-all-start
  25.7 17.4 %all-to-all-done = bf16[8,8,16,384]{3,2,1,0:T(8,128)(2,1)S(1)} async-done(((bf16[8,8,16,384]{3,2,1,0:T(8,128)(2,1)}), bf16[8,8,16,384]{3,2,1,0:T(8,128)(2,1)S(1)}, u32[]{:S(2)}, u32[]{:S(2)}) %all-to-all-start) | async-done | bytes 786464 | tf_op jit(solution)/shard_map/all_to_all | solution.py:88
  49.2 2.3 copy.100
  57.4 7.1 all-to-all-start.2
  67.1 2.5 copy.126
  69.6 12.4 %all-to-all-done.2 = bf16[1,8,128,384]{3,1,0,2:T(8,128)(2,1)S(1)} async-done(((bf16[1,8,128,384]{3,1,0,2:T(8,128)(2,1)}), bf16[1,8,128,384]{3,1,0,2:T(8,128)(2,1)S(1)}, u32[]{:S(2)}, u32[]{:S(2)}) %all-to-all-start.2) | async-done | bytes 786464 | tf_op jit(solution)/shard_map/all_to_all | solution.py:114
  85.3 2.6 copy.127
  87.9 5.7 fusion.17
  93.6 224.6 %pmax.7 = bf16[16,8,64]{2,1,0:T(8,128)(2,1)} all-reduce(bf16[16,8,64]{2,1,0:T(8,128)(2,1)} %get-tuple-element.22), channel_id=1, replica_groups=mesh['trk'=32,'frm'=8] {'trk'}, use_global_device_ids=true, to_apply=%region_9.0 | all-reduce | flops 8192 | bytes 32768 | tf_op jit(solution)/shard_map/pmax | solution.py:130
  321.3 4.9 fusion.84
  327.0 3.5 fusion.22
  330.5 218.5 %psum.15 = bf16[16,64,8]{1,2,0:T(8,128)(2,1)S(1)} all-reduce(bf16[16,64,8]{1,2,0:T(8,128)(2,1)S(1)} %bitcast.130), channel_id=1, replica_groups=mesh['trk'=32,'frm'=8] {'trk'}, use_global_device_ids=true, to_apply=%region_12.0 | all-reduce | flops 8192 | bytes 32768 | tf_op jit(solution)/shard_map/psum | solution.py:138
  549.7 1.7 fusion.90
  551.4 1.7 copy.132
  553.1 202.8 %all-reduce.2.cloned.1.call-done = bf16[16,64,8,48]{1,3,2,0:T(8,128)(2,1)} async-done(((bf16[16,64,8,48]{1,3,2,0:T(8,128)(2,1)}), bf16[16,64,8,48]{1,3,2,0:T(8,128)(2,1)}) %all-reduce.2.cloned.1.call-update) | async-done | bytes 786448 | tf_op jit(solution)/shard_map/psum | solution.py:137
  755.9 1.9 divide_convert_fusion
  759.3 5.5 convert_reduce_fusion.5
  766.0 2.1 convolution_convert_fusion.1
  770.9 2.6 copy.128
  773.4 2.4 multiply_reduce_fusion
  778.3 1.8 copy.119
  780.1 1.9 convert_reduce_fusion
  782.5 6.1 fusion.80
  (89 shorter events, 37.8 us)
Async XLA Ops:
  7.2 752.1 %copy-start = (bf16[1536,384]{1,0:T(8,128)(2,1)S(1)}, bf16[1536,384]{1,0:T(8,128)(2,1)}, u32[]{:S(2)}) copy-start(bf16[1536,384]{1,0:T(8,128)(2,1)} %param.31) | copy-start | bytes 3538948
  7.2 12.1 %copy-start.1 = (bf16[64,16,384]{2,1,0:T(8,128)(2,1)S(1)}, bf16[64,16,384]{2,1,0:T(8,128)(2,1)}, u32[]{:S(2)}) copy-start(bf16[64,16,384]{2,1,0:T(8,128)(2,1)} %param.16) | copy-start | bytes 2359300
  8.7 11.8 %all-to-all-start.1 = ((bf16[8,8,16]{2,1,0:T(8,128)(2,1)}), bf16[8,8,16]{2,1,0:T(8,128)(2,1)S(1)}, u32[]{:S(2)}, u32[]{:S(2)}) async-start(bf16[8,8,16]{2,1,0:T(8,128)(2,1)} %bitcast.8), calls=%async_computation.1 | async-start | bytes 32768 | tf_op jit(solution)/shard_map/all_to_all | solution.py:95
  20.5 22.6 %all-to-all-start = ((bf16[8,8,16,384]{3,2,1,0:T(8,128)(2,1)}), bf16[8,8,16,384]{3,2,1,0:T(8,128)(2,1)S(1)}, u32[]{:S(2)}, u32[]{:S(2)}) async-start(bf16[8,8,16,384]{3,2,1,0:T(8,128)(2,1)} %bitcast), calls=%async_computation | async-start | bytes 1572864 | tf_op jit(solution)/shard_map/all_to_all | solution.py:88
  43.1 1.2 copy-start.15
  52.7 1.2 copy-start.6
  54.0 1.4 copy-start.8
  56.1 8.4 %copy-start.2 = (bf16[16,64,384]{2,1,0:T(8,128)(2,1)S(1)}, bf16[16,64,384]{2,1,0:T(8,128)(2,1)}, u32[]{:S(2)}) copy-start(bf16[16,64,384]{2,1,0:T(8,128)(2,1)} %param.18) | copy-start | bytes 2359300
  57.4 7.8 copy-start.14
  57.4 24.6 %all-to-all-start.2 = ((bf16[1,8,128,384]{3,1,0,2:T(8,128)(2,1)}), bf16[1,8,128,384]{3,1,0,2:T(8,128)(2,1)S(1)}, u32[]{:S(2)}, u32[]{:S(2)}) async-start(bf16[1,8,128,384]{3,1,0,2:T(8,128)(2,1)} %copy.107), calls=%async_computation.2 | async-start | bytes 1572864 | tf_op jit(solution)/shard_map/all_to_all | solution.py:114
  64.5 691.4 %all-reduce.2.cloned.1.call-start = ((), (), s32[]{:S(2)}) async-start(), calls=%async_computation.3 | async-start | bytes 3145728 | tf_op jit(solution)/shard_map/psum | solution.py:137
  64.5 1.0 copy-start.17
  82.1 0.8 copy-start.13
  82.2 1.1 copy-start.16
  82.5 1.8 copy-start.10
  82.9 1.4 copy-start.11
  326.2 0.8 copy-start.7
  755.9 2.0 copy-start.9
  764.8 3.3 copy-start.5
  770.8 2.6 copy-start.3
  775.8 1.4 copy-start.4
  780.1 2.4 copy-start.12
Sparse Core Ops, SparseCore 0:
  326.3 429.5 all-reduce.1
where the time goes:
time: 797 us; the launch traced here: 795 us
  blocking collectives  443 us (56%)
  waiting for transfers between devices  233 us (29%)
  matrix products  39.7 us (5%)
  local copies, waits for them, and re-layouts  28.8 us (4%)
  other arithmetic  18.6 us (2%)
  starting transfers between devices  18.2 us (2%)
  between operations  14.5 us (2%)
    pmax x1, blocking collectives, shards(): lax.pmax(jnp.max(scores, axis=-1).astype(jnp.bfloat16), 'trk')  225 us
    psum x1, blocking collectives, shards(): lax.psum(totals.astype(jnp.bfloat16), 'trk').astype(jnp.float32)  219 us
    psum x1, waiting for transfers between devices, shards(): lax.psum(numer.astype(jnp.bfloat16), 'trk').astype(jnp.float32)  203 us
    all_to_all x1, waiting for transfers between devices, shards(): lax.all_to_all(normed.reshape(frm_count, per_group, frm_rows, model_width...  17.4 us
  transfers between devices with their start and end apart: 4, of which 3 were waited for; matrix products, arithmetic and copies ran while one was open for 2% of the time, Pallas kernels for 0%

commit v1 on v0

v1 whole, which is shorter than its diff:
```python
import functools
import math

import jax
import jax.numpy as jnp
from jax import lax
from jax.experimental import pallas as pl
from jax.experimental.pallas import tpu as pltpu
from jax.sharding import PartitionSpec as P

HEADS = 8
HEAD = 48
SLOT = 64
TILE = 128
PAIRS = HEADS // 2
WIDE = HEADS * SLOT
PENALTY = 4.0
EPSILON = 1e-05
SCALE = 1.0 / math.sqrt(HEAD)
MESH = pl.DeviceIdType.MESH
f32 = jnp.float32
bf16 = jnp.bfloat16


def dot(a, b):
    return lax.dot_general(a, b, (((1,), (0,)), ((), ())), preferred_element_type=f32)


def dot_t(a, b):
    return lax.dot_general(a, b, (((1,), (1,)), ((), ())), preferred_element_type=f32)


def unit(x):
    center = x - jnp.mean(x, axis=-1, keepdims=True)
    spread = jnp.mean(center * center, axis=-1, keepdims=True)
    return center * lax.rsqrt(spread + EPSILON)


def gelu(x):
    return jax.nn.gelu(x, approximate=True)


def spread_matrix(rows_are_padded):
    shape = (WIDE, HEADS * HEAD) if rows_are_padded else (HEADS * HEAD, WIDE)
    tight = lax.broadcasted_iota(jnp.int32, shape, 1 if rows_are_padded else 0)
    padded = lax.broadcasted_iota(jnp.int32, shape, 0 if rows_are_padded else 1)
    target = tight
    for h in range(1, HEADS):
        target = target + jnp.where(tight >= HEAD * h, SLOT - HEAD, 0)
    return jnp.where(target == padded, 1.0, 0.0).astype(bf16)


def halves(x, lane):
    zero = jnp.zeros_like(x)
    return jnp.concatenate(
        [jnp.where(lane < SLOT, x, zero), jnp.where(lane < SLOT, zero, x)], axis=0
    )


def lanes(rows):
    return lax.broadcasted_iota(jnp.int32, (rows, TILE), 1)


def slot_lanes(rows):
    lane = lanes(rows)
    return jnp.where(lane < SLOT, lane, lane - SLOT)


def pair_attention(q, k, v, bias):
    lane_k, lane_q = lanes(k.shape[0]), lanes(q.shape[0])
    v = jnp.where(slot_lanes(v.shape[0]) == HEAD, jnp.ones_like(v), v)
    s = dot_t(q, halves(k, lane_k)) * SCALE
    if bias is not None:
        s = s + bias
    low = jnp.full_like(s, -jnp.inf)
    first = jnp.max(jnp.where(lane_q < SLOT, s, low), axis=-1, keepdims=True)
    second = jnp.max(jnp.where(lane_q < SLOT, low, s), axis=-1, keepdims=True)
    peak = jnp.where(lane_q < SLOT, first, second)
    e = jnp.exp(s - peak).astype(bf16)
    return dot(e, halves(v, lane_k)), peak


def with_peak(num, peak):
    place = slot_lanes(num.shape[0])
    high = peak.astype(bf16).astype(f32)
    rest = peak - high
    mid = rest.astype(bf16).astype(f32)
    low = rest - mid
    num = jnp.where(place == HEAD + 1, high, num)
    num = jnp.where(place == HEAD + 2, mid, num)
    num = jnp.where(place == HEAD + 3, low, num)
    return num.astype(bf16)


def over_den(num):
    rows = num.shape[0]
    den = jnp.where(lanes(rows) < SLOT, num[:, HEAD : HEAD + 1], num[:, SLOT + HEAD : SLOT + HEAD + 1])
    return jnp.where(slot_lanes(rows) < HEAD, num / den, 0.0).astype(bf16)


def merge(ref, pair):
    count, rows = ref.shape[0], ref.shape[1]
    part = ref[:, :, pair * TILE : (pair + 1) * TILE]
    flat = part.reshape(count * rows, TILE)
    row = lax.broadcasted_iota(jnp.int32, (TILE, TILE), 0)
    col = lax.broadcasted_iota(jnp.int32, (TILE, TILE), 1)
    same = (row < SLOT) == (col < SLOT)
    place = jnp.where(row < SLOT, row, row - SLOT)
    pick = same & (place > HEAD) & (place < HEAD + 4)
    peaks = dot(flat, jnp.where(pick, 1.0, 0.0).astype(bf16)).reshape(count, rows, TILE)
    peak = jnp.max(peaks, axis=0)
    total = jnp.sum(jnp.exp(peaks - peak[None]) * part.astype(f32), axis=0)
    return total, peak


def kernel(
    dims,
    tokens,
    vis,
    read_bias,
    virtual,
    gains,
    w_time_qkv,
    w_time_o,
    w_read_q,
    w_read_kv,
    w_read_o,
    w_write_q,
    w_write_kv,
    w_write_o,
    w_up,
    w_down,
    v_up,
    v_down,
    track_out,
    virt_out,
    tok,
    x_recv,
    stage,
    y_recv,
    vis_recv,
    time_bias,
    y1t,
    y1,
    virt,
    vq,
    kv2,
    wq,
    part_send,
    part_recv,
    cross,
    vout,
    outt,
    raw,
    r_up,
    r_down,
    r_vup,
    r_vdown,
    p_time_qkv,
    p_time_o,
    p_read_q,
    p_read_kv,
    p_read_o,
    p_write_q,
    p_write_kv,
    p_write_o,
    load_sem,
    own_sem,
    vis_sem,
    tok_sem,
    back_sem,
    part_sem,
    cross_sem,
    gather_sem,
    out_sem,
):
    nfrm, nplane, chunks, per, frames = dims
    trk, me = lax.axis_index("trk"), lax.axis_index("frm")
    spot, half = lax.div(trk, 2), lax.rem(trk, 2)
    width = HEADS * HEAD
    group = min(4, frames)

    def column(k):
        return lax.rem(me + k, nfrm)

    def plane(i):
        return lax.rem(spot + i, nplane)

    weights = (w_time_qkv, w_time_o, w_read_q, w_read_kv, w_read_o, w_write_q, w_write_kv, w_write_o)
    offsets = []
    at = 0
    loads = []
    for n, w in enumerate(weights):
        cols = w.shape[1]
        offsets.append((at, cols))
        loads.append(pltpu.make_async_copy(w, raw.at[:, pl.ds(at, cols)], load_sem.at[n]))
        at += cols
    for w, dst in ((w_up, r_up), (w_down, r_down), (v_up, r_vup), (v_down, r_vdown), (virtual, virt), (tokens, tok)):
        loads.append(pltpu.make_async_copy(w, dst, load_sem.at[len(loads)]))
    own = pltpu.make_async_copy(tokens.at[me], x_recv.at[me], own_sem)

    barrier = pltpu.get_barrier_semaphore()

    def greet_column(k, carry):
        pl.semaphore_signal(barrier, inc=1, device_id=(trk, column(k)), device_id_type=MESH)
        return carry

    def greet_plane(i, carry):
        pl.semaphore_signal(barrier, inc=1, device_id=(plane(i) * 2 + half, me), device_id_type=MESH)
        return carry

    lax.fori_loop(1, nfrm, greet_column, 0)
    lax.fori_loop(1, nplane, greet_plane, 0)
    partner = trk + 1 - 2 * half
    pl.semaphore_signal(barrier, inc=1, device_id=(partner, me), device_id_type=MESH)
    own.start()
    for load in loads:
        load.start()
    pl.semaphore_wait(barrier, nfrm - 1 + nplane - 1 + 1)

    def vis_copy(k):
        return pltpu.make_async_remote_copy(
            src_ref=vis.at[column(k)],
            dst_ref=vis_recv.at[me],
            send_sem=vis_sem.at[0, k],
            recv_sem=vis_sem.at[1, k],
            device_id=(trk, column(k)),
            device_id_type=MESH,
        )

    def tok_copy(c, k):
        return pltpu.make_async_remote_copy(
            src_ref=tokens.at[column(k), c],
            dst_ref=x_recv.at[me, c],
            send_sem=tok_sem.at[0, c, k],
            recv_sem=tok_sem.at[1, c, k],
            device_id=(trk, column(k)),
            device_id_type=MESH,
        )

    def back_copy(c, k):
        return pltpu.make_async_remote_copy(
            src_ref=stage.at[c, column(k)],
            dst_ref=y_recv.at[me, c],
            send_sem=back_sem.at[0, c, k],
            recv_sem=back_sem.at[1, c, k],
            device_id=(trk, column(k)),
            device_id_type=MESH,
        )

    def each_peer(act):
        def body(k, carry):
            act(k)
            return carry

        lax.fori_loop(1, nfrm, body, 0)

    each_peer(lambda k: vis_copy(k).start())

    def send_chunk(c, carry):
        each_peer(lambda k: tok_copy(c, k).start())
        return carry

    lax.fori_loop(0, chunks, send_chunk, 0)

    for load in loads:
        load.wait()
    cols_to = spread_matrix(False)
    rows_to = spread_matrix(True)

    def pad_cols(n, dst):
        start, cols = offsets[n]
        for b in range(cols // width):
            block = raw[:, start + b * width : start + (b + 1) * width]
            dst[:, b * WIDE : (b + 1) * WIDE] = dot(block, cols_to).astype(bf16)

    def pad_rows(n, dst):
        start, cols = offsets[n]
        dst[...] = dot(rows_to, raw[:, start : start + cols]).astype(bf16)

    pad_cols(0, p_time_qkv)
    pad_rows(1, p_time_o)
    pad_cols(2, p_read_q)
    pad_cols(3, p_read_kv)
    pad_rows(4, p_read_o)
    pad_cols(5, p_write_q)
    pad_cols(6, p_write_kv)
    pad_rows(7, p_write_o)

    virtuals = virt.shape[1]

    def queries(g, carry):
        rows = virt[pl.ds(g * group, group)].reshape(group * virtuals, width).astype(f32)
        normed = (unit(rows) * gains[4:5, :]).astype(bf16)
        vq[pl.ds(g * group, group)] = dot(normed, p_read_q[...]).astype(bf16).reshape(group, virtuals, WIDE)
        return carry

    lax.fori_loop(0, frames // group, queries, 0)

    each_peer(lambda k: vis_copy(k).wait_recv())
    vis_recv[pl.ds(me, 1)] = vis[pl.ds(me, 1)]
    row_bias = jnp.concatenate([vis_recv[s] for s in range(nfrm)], axis=-1)
    time_bias[...] = (row_bias.astype(f32) - 1.0) * PENALTY
    own.wait()
    keys = nfrm * frames

    def attend_chunk(c, carry):
        each_peer(lambda k: tok_copy(c, k).wait_recv())
        rows = jnp.concatenate(
            [x_recv[:, c, t].reshape(keys, width) for t in range(per)], axis=0
        )
        normed = (unit(rows.astype(f32)) * gains[0:1, :]).astype(bf16)
        triple = dot(normed, p_time_qkv[...]).astype(bf16)
        lane = lanes(keys)
        outs = []
        for t in range(per):
            bias = time_bias[pl.ds(c * per + t, 1), :]
            tiles = []
            for p in range(PAIRS):
                q, k, v = (
                    triple[t * keys : (t + 1) * keys, n * WIDE + p * TILE : n * WIDE + (p + 1) * TILE]
                    for n in range(3)
                )
                s = dot_t(q, halves(k, lane)) * SCALE
                parts, dens = [], []
                for h in range(2):
                    sh = s[:, h * keys : (h + 1) * keys] + bias
                    e = jnp.exp(sh - jnp.max(sh, axis=-1, keepdims=True))
                    dens.append(jnp.sum(e, axis=-1, keepdims=True))
                    parts.append(e.astype(bf16))
                num = dot(jnp.concatenate(parts, axis=-1), halves(v, lane))
                tiles.append((num / jnp.where(lane < SLOT, dens[0], dens[1])).astype(bf16))
            outs.append(jnp.concatenate(tiles, axis=-1))
        projected = dot(jnp.concatenate(outs, axis=0), p_time_o[...]).astype(bf16)
        for t in range(per):
            stage[c, :, t] = projected[t * keys : (t + 1) * keys].reshape(nfrm, frames, width)
        each_peer(lambda k: back_copy(c, k).start())
        y_recv[pl.ds(me, 1), pl.ds(c, 1)] = stage[pl.ds(c, 1), pl.ds(me, 1)]
        return carry

    lax.fori_loop(0, chunks, attend_chunk, 0)

    def add_chunk(c, carry):
        each_peer(lambda k: back_copy(c, k).wait_recv())
        for o in range(nfrm):
            total = tok[o, c].astype(f32) + y_recv[o, c].astype(f32)
            total = total.astype(bf16).astype(f32).reshape(per * frames, width)
            start = pl.multiple_of((o * chunks + c) * (per * frames), per * frames)
            for n in range(width // TILE):
                y1t[n, pl.ds(start, per * frames), :] = total[:, n * TILE : (n + 1) * TILE]
        return carry

    lax.fori_loop(0, chunks, add_chunk, 0)
    tracks = y1.shape[1]

    def read_keys(g, carry):
        rows = []
        for n in range(group):
            f = g * group + n
            rows.append(
                jnp.concatenate(
                    [y1t[m, pl.ds(f, tracks, stride=frames), :] for m in range(width // TILE)], axis=-1
                )
            )
        rows = jnp.concatenate(rows, axis=0)
        y1[pl.ds(g * group, group)] = rows.astype(bf16).reshape(group, tracks, width)
        normed = (unit(rows) * gains[1:2, :]).astype(bf16)
        kv2[pl.ds(g * group, group)] = dot(normed, p_read_kv[...]).astype(bf16).reshape(group, tracks, 2 * WIDE)
        return carry

    lax.fori_loop(0, frames // group, read_keys, 0)

    def part_copy(i):
        return pltpu.make_async_remote_copy(
            src_ref=part_send.at[plane(i)],
            dst_ref=part_recv.at[spot],
            send_sem=part_sem.at[0, i],
            recv_sem=part_sem.at[1, i],
            device_id=(plane(i) * 2 + half, me),
            device_id_type=MESH,
        )

    def read_frame(f):
        bias = read_bias[pl.ds(f, 1), :]
        tiles = []
        for p in range(PAIRS):
            at = p * TILE
            num, peak = pair_attention(
                vq[f, :, at : at + TILE], kv2[f, :, at : at + TILE], kv2[f, :, WIDE + at : WIDE + at + TILE], bias
            )
            tiles.append(with_peak(num, peak))
        return jnp.concatenate(tiles, axis=-1)

    def read_step(i, carry):
        part_send[plane(i)] = read_frame(plane(i))
        part_copy(i).start()
        return carry

    lax.fori_loop(1, nplane, read_step, 0)
    part_recv[spot] = read_frame(spot)

    def write_queries(g, carry):
        rows = y1[pl.ds(g * group, group)].reshape(group * tracks, width).astype(f32)
        normed = (unit(rows) * gains[2:3, :]).astype(bf16)
        wq[pl.ds(g * group, group)] = dot(normed, p_write_q[...]).astype(bf16).reshape(group, tracks, WIDE)
        return carry

    lax.fori_loop(0, frames // group, write_queries, 0)

    def each_in_plane(act):
        def body(i, carry):
            act(i)
            return carry

        lax.fori_loop(1, nplane, body, 0)

    each_in_plane(lambda i: part_copy(i).wait_recv())
    for p in range(PAIRS):
        total, peak = merge(part_recv, p)
        cross[pl.ds(half, 1), :, p * TILE : (p + 1) * TILE] = with_peak(total, peak)[None]
    across = pltpu.make_async_remote_copy(
        src_ref=cross.at[half],
        dst_ref=cross.at[half],
        send_sem=cross_sem.at[0],
        recv_sem=cross_sem.at[1],
        device_id=(partner, me),
        device_id_type=MESH,
    )
    across.start()
    across.wait_recv()
    readout = jnp.concatenate([over_den(merge(cross, p)[0]) for p in range(PAIRS)], axis=-1)

    virt1 = (virt[spot].astype(f32) + dot(readout, p_read_o[...])).astype(bf16).astype(f32)
    normed = (unit(virt1) * gains[5:6, :]).astype(bf16)
    middle = gelu(dot(normed, r_vup[...])).astype(bf16)
    vout[spot] = (virt1 + dot(middle, r_vdown[...])).astype(bf16)

    def gather_copy(i):
        return pltpu.make_async_remote_copy(
            src_ref=vout.at[spot],
            dst_ref=vout.at[spot],
            send_sem=gather_sem.at[0, i],
            recv_sem=gather_sem.at[1, i],
            device_id=(plane(i) * 2 + half, me),
            device_id_type=MESH,
        )

    each_in_plane(lambda i: gather_copy(i).start())

    def write_group(g, carry):
        for n in range(group):
            i = g * group + n

            @pl.when(i > 0)
            def _():
                gather_copy(i).wait_recv()

        where = [lax.rem(spot - (g * group + n) + nplane, nplane) for n in range(group)]
        rows = jnp.concatenate([vout[f] for f in where], axis=0).astype(f32)
        normed = (unit(rows) * gains[6:7, :]).astype(bf16)
        pairs = dot(normed, p_write_kv[...]).astype(bf16)
        outs = []
        for n, f in enumerate(where):
            tiles = []
            for p in range(PAIRS):
                at = p * TILE
                block = pairs[n * virtuals : (n + 1) * virtuals]
                num, _ = pair_attention(
                    wq[f, :, at : at + TILE], block[:, at : at + TILE], block[:, WIDE + at : WIDE + at + TILE], None
                )
                tiles.append(over_den(num))
            outs.append(jnp.concatenate(tiles, axis=-1))
        first = jnp.concatenate([y1[f] for f in where], axis=0).astype(f32)
        second = first + dot(jnp.concatenate(outs, axis=0), p_write_o[...])
        second = second.astype(bf16).astype(f32)
        normed = (unit(second) * gains[3:4, :]).astype(bf16)
        middle = gelu(dot(normed, r_up[...])).astype(bf16)
        final = second + dot(middle, r_down[...])
        for n, f in enumerate(where):
            for m in range(width // TILE):
                outt[m, pl.ds(f, tracks, stride=frames), :] = final[
                    n * tracks : (n + 1) * tracks, m * TILE : (m + 1) * TILE
                ]
        return carry

    lax.fori_loop(0, frames // group, write_group, 0)
    virt_done = pltpu.make_async_copy(vout, virt_out, out_sem)
    virt_done.start()
    block = tracks // 8

    def finish(b, carry):
        rows = pl.multiple_of(b * (block * frames), block * frames)
        for m in range(width // TILE):
            part = outt[m, pl.ds(rows, block * frames), :].astype(bf16)
            track_out[pl.ds(b * block, block), :, m * TILE : (m + 1) * TILE] = part.reshape(block, frames, TILE)
        return carry

    lax.fori_loop(0, 8, finish, 0)

    each_peer(lambda k: vis_copy(k).wait_send())

    def drain(c, carry):
        each_peer(lambda k: tok_copy(c, k).wait_send())
        each_peer(lambda k: back_copy(c, k).wait_send())
        return carry

    lax.fori_loop(0, chunks, drain, 0)
    each_in_plane(lambda i: part_copy(i).wait_send())
    across.wait_send()
    each_in_plane(lambda i: gather_copy(i).wait_send())
    virt_done.wait()


def shards(tokens, visible, virtual, gains, *weights):
    tracks, frames, width = tokens.shape
    nfrm, nplane = lax.axis_size("frm"), lax.axis_size("trk") // 2
    virtuals = virtual.shape[1]
    owned = tracks // nfrm
    chunks = 4
    per = owned // chunks
    hidden = weights[8].shape[1]
    dims = (nfrm, nplane, chunks, per, frames)
    cut = tokens.reshape(nfrm, chunks, per, frames, width)
    bias = ((visible.astype(f32) - 1.0) * PENALTY).T
    bias = jnp.concatenate([bias, bias], axis=1)
    narrow = (nfrm, chunks, per, frames, width)
    vmem, anywhere = pl.BlockSpec(memory_space=pltpu.VMEM), pl.BlockSpec(memory_space=pl.ANY)
    dma = pltpu.SemaphoreType.DMA
    raw_cols = sum(w.shape[1] for w in weights[:8])
    out = pl.pallas_call(
        functools.partial(kernel, dims),
        out_shape=(
            jax.ShapeDtypeStruct((tracks, frames, width), bf16),
            jax.ShapeDtypeStruct((frames, virtuals, width), bf16),
        ),
        in_specs=[anywhere, vmem, vmem, anywhere, vmem] + [anywhere] * 12,
        out_specs=(vmem, anywhere),
        scratch_shapes=[
            pltpu.VMEM(narrow, bf16),
            pltpu.VMEM(narrow, bf16),
            pltpu.VMEM((chunks, nfrm, per, frames, width), bf16),
            pltpu.VMEM(narrow, bf16),
            pltpu.VMEM((nfrm, owned, frames), jnp.int32),
            pltpu.VMEM((owned, nfrm * frames), f32),
            pltpu.VMEM((width // TILE, tracks * frames, TILE), f32),
            pltpu.VMEM((frames, tracks, width), bf16),
            pltpu.VMEM((frames, virtuals, width), bf16),
            pltpu.VMEM((frames, virtuals, WIDE), bf16),
            pltpu.VMEM((frames, tracks, 2 * WIDE), bf16),
            pltpu.VMEM((frames, tracks, WIDE), bf16),
            pltpu.VMEM((nplane, virtuals, WIDE), bf16),
            pltpu.VMEM((nplane, virtuals, WIDE), bf16),
            pltpu.VMEM((2, virtuals, WIDE), bf16),
            pltpu.VMEM((frames, virtuals, width), bf16),
            pltpu.VMEM((width // TILE, tracks * frames, TILE), f32),
            pltpu.VMEM((width, raw_cols), bf16),
            pltpu.VMEM((width, hidden), bf16),
            pltpu.VMEM((hidden, width), bf16),
            pltpu.VMEM((width, hidden), bf16),
            pltpu.VMEM((hidden, width), bf16),
            pltpu.VMEM((width, 3 * WIDE), bf16),
            pltpu.VMEM((WIDE, width), bf16),
            pltpu.VMEM((width, WIDE), bf16),
            pltpu.VMEM((width, 2 * WIDE), bf16),
            pltpu.VMEM((WIDE, width), bf16),
            pltpu.VMEM((width, WIDE), bf16),
            pltpu.VMEM((width, 2 * WIDE), bf16),
            pltpu.VMEM((WIDE, width), bf16),
            dma((14,)),
            dma,
            dma((2, nfrm)),
            dma((2, chunks, nfrm)),
            dma((2, chunks, nfrm)),
            dma((2, nplane)),
            dma((2,)),
            dma((2, nplane)),
            dma,
        ],
        compiler_params=pltpu.CompilerParams(
            collective_id=0, has_side_effects=True, vmem_limit_bytes=56 * 1024 * 1024
        ),
    )(cut, visible.reshape(nfrm, owned, frames), bias, virtual, gains, *weights)
    return out


def solution(mesh):
    in_specs = (P("trk", "frm", None), P("trk", "frm"), P("frm", None, None)) + (P(),) * 13
    out_specs = (P("trk", "frm", None), P("frm", None, None))
    return jax.shard_map(shards, mesh=mesh, in_specs=in_specs, out_specs=out_specs, check_vma=False)
```

time: 797 us -> 125 us (0.16)
  the two profiles are of different devices: /device:TPU:32 before, /device:TPU:8 now
where the time goes in v1:
time: 125 us
  Pallas kernels  118 us (94%)
  local copies, waits for them, and re-layouts  4.44 us (4%)
  other arithmetic  1.38 us (1%)
    pallas_call x1, Pallas kernels, shards(): pl.pallas_call(functools.partial(kernel, dims), out_shape=(jax.ShapeDtype...  118 us
    unnamed x5, local copies, waits for them, and re-layouts  4.44 us

profile of v1, /device:TPU:8, one launch (start us, length us, event | category | flops | bytes accessed | tf_op | source)
XLA Modules:
  0.0 124.9 jit_solution(5281646065494059103)
XLA Ops:
  0.6 0.7 multiply_bitcast_fusion
  1.3 0.7 pad_maximum_fusion.read_bias
  2.0 1.4 %copy.18 = s32[64,16]{1,0:T(8,128)} copy(s32[64,16]{0,1:T(8,128)} %param.17) | data formatting | bytes 8192 | tf_op args[1]
  3.4 118.5 %shard_map.167 = (bf16[64,16,384]{2,1,0:T(8,128)(2,1)}, bf16[16,64,384]{2,1,0:T(8,128)(2,1)}) custom-call(bf16[8,4,2,16,384]{4,3,2,1,0:T(8,128)(2,1)} %bitcast.4, s32[8,8,16]{2,1,0:T(8,128)} %bitcast.5, f32[16,128]{1,0:T(8,128)} %pad_maximum_fusion.read_bias, bf16[16,64,384]{2,1,0:T(8,128)(2,1)} %virtual.1, f32[7,384]{1,0:T(8,128)} %gains.1, ...), custom_call_target="tpu_custom_call" | custom-call | tf_op jit(solution)/shard_map/pallas_call | solution.py:530
  121.9 0.0 copy-start
  121.9 2.2 %copy.21 = bf16[64,16,384]{2,1,0:T(8,128)(2,1)} copy(bf16[64,16,384]{2,1,0:T(8,128)(2,1)} %get-tuple-element.4) | data formatting | bytes 1572864
  124.0 0.0 copy-done
  124.1 0.9 copy.22
Async XLA Ops:
  121.9 2.2 %copy-start = (bf16[16,64,384]{2,1,0:T(8,128)(2,1)S(1)}, bf16[16,64,384]{2,1,0:T(8,128)(2,1)}, u32[]{:S(2)}) copy-start(bf16[16,64,384]{2,1,0:T(8,128)(2,1)} %get-tuple-element.5) | copy-start | bytes 2359300

commit v2 on v1

v2 whole, which is shorter than its diff:
```python
import functools
import math

import jax
import jax.numpy as jnp
from jax import lax
from jax.experimental import pallas as pl
from jax.experimental.pallas import tpu as pltpu
from jax.sharding import PartitionSpec as P

HEADS = 8
HEAD = 48
SLOT = 64
TILE = 128
PAIRS = HEADS // 2
WIDE = HEADS * SLOT
PENALTY = 4.0
EPSILON = 1e-05
SCALE = 1.0 / math.sqrt(HEAD)
MESH = pl.DeviceIdType.MESH
f32 = jnp.float32
bf16 = jnp.bfloat16


def dot(a, b):
    return lax.dot_general(a, b, (((1,), (0,)), ((), ())), preferred_element_type=f32)


def dot_t(a, b):
    return lax.dot_general(a, b, (((1,), (1,)), ((), ())), preferred_element_type=f32)


def unit(x):
    center = x - jnp.mean(x, axis=-1, keepdims=True)
    spread = jnp.mean(center * center, axis=-1, keepdims=True)
    return center * lax.rsqrt(spread + EPSILON)


def gelu(x):
    return jax.nn.gelu(x, approximate=True)


def spread_matrix(rows_are_padded):
    shape = (WIDE, HEADS * HEAD) if rows_are_padded else (HEADS * HEAD, WIDE)
    tight = lax.broadcasted_iota(jnp.int32, shape, 1 if rows_are_padded else 0)
    padded = lax.broadcasted_iota(jnp.int32, shape, 0 if rows_are_padded else 1)
    target = tight
    for h in range(1, HEADS):
        target = target + jnp.where(tight >= HEAD * h, SLOT - HEAD, 0)
    return jnp.where(target == padded, 1.0, 0.0).astype(bf16)


def halves(x, lane):
    zero = jnp.zeros_like(x)
    return jnp.concatenate(
        [jnp.where(lane < SLOT, x, zero), jnp.where(lane < SLOT, zero, x)], axis=0
    )


def lanes(rows):
    return lax.broadcasted_iota(jnp.int32, (rows, TILE), 1)


def slot_lanes(rows):
    lane = lanes(rows)
    return jnp.where(lane < SLOT, lane, lane - SLOT)


def pair_attention(qs, ks, vs, biases):
    lane_k, lane_q = lanes(ks[0].shape[0]), lanes(qs[0].shape[0])
    marked = slot_lanes(ks[0].shape[0]) == HEAD
    vs = [jnp.where(marked, jnp.ones_like(v), v) for v in vs]
    scores = [dot_t(q, halves(k, lane_k)) * SCALE for q, k in zip(qs, ks)]
    if biases is not None:
        scores = [s + b for s, b in zip(scores, biases)]
    left = lane_q < SLOT
    first = [jnp.max(jnp.where(left, s, -jnp.inf), axis=-1, keepdims=True) for s in scores]
    second = [jnp.max(jnp.where(left, -jnp.inf, s), axis=-1, keepdims=True) for s in scores]
    peaks = [jnp.where(left, x, y) for x, y in zip(first, second)]
    expos = [jnp.exp(s - p).astype(bf16) for s, p in zip(scores, peaks)]
    return [dot(e, halves(v, lane_k)) for e, v in zip(expos, vs)], peaks


def with_peak(num, peak):
    place = slot_lanes(num.shape[0])
    high = peak.astype(bf16).astype(f32)
    rest = peak - high
    mid = rest.astype(bf16).astype(f32)
    low = rest - mid
    num = jnp.where(place == HEAD + 1, high, num)
    num = jnp.where(place == HEAD + 2, mid, num)
    num = jnp.where(place == HEAD + 3, low, num)
    return num.astype(bf16)


def over_den(num):
    rows = num.shape[0]
    den = jnp.where(lanes(rows) < SLOT, num[:, HEAD : HEAD + 1], num[:, SLOT + HEAD : SLOT + HEAD + 1])
    return jnp.where(slot_lanes(rows) < HEAD, num / den, 0.0).astype(bf16)


def merge(part):
    count, rows = part.shape[0], part.shape[1]
    row = lax.broadcasted_iota(jnp.int32, (TILE, TILE), 0)
    col = lax.broadcasted_iota(jnp.int32, (TILE, TILE), 1)
    same = (row < SLOT) == (col < SLOT)
    place = jnp.where(row < SLOT, row, row - SLOT)
    pick = same & (place > HEAD) & (place < HEAD + 4)
    peaks = dot(part.reshape(count * rows, TILE), jnp.where(pick, 1.0, 0.0).astype(bf16))
    peaks = peaks.reshape(count, rows, TILE)
    peak = jnp.max(peaks, axis=0)
    total = jnp.sum(jnp.exp(peaks - peak[None]) * part.astype(f32), axis=0)
    return total, peak


def merge_tiles(value):
    return jnp.concatenate(
        [
            with_peak(*merge(value[:, :, at : at + TILE]))
            for at in range(0, value.shape[-1], TILE)
        ],
        axis=-1,
    )


def kernel(
    dims,
    tokens,
    vis,
    virtual,
    gains,
    w_time_qkv,
    w_time_o,
    w_read_q,
    w_read_kv,
    w_read_o,
    w_write_q,
    w_write_kv,
    w_write_o,
    w_up,
    w_down,
    v_up,
    v_down,
    track_out,
    virt_out,
    tok,
    x_recv,
    qkv,
    stage,
    y_recv,
    vis_recv,
    time_bias,
    read_bias,
    y1t,
    y1,
    virt,
    vq,
    kv2,
    wq,
    pay,
    one_x,
    one_y,
    mid_x,
    mid_y,
    two_x,
    two_y,
    cross,
    vout,
    outv,
    raw,
    r_up,
    r_down,
    r_vup,
    r_vdown,
    p_time_qkv,
    p_time_o,
    p_read_q,
    p_read_kv,
    p_read_o,
    p_write_q,
    p_write_kv,
    p_write_o,
    load_sem,
    own_sem,
    vis_sem,
    tok_sem,
    back_sem,
    part_sem,
    cross_sem,
    gather_sem,
    out_sem,
):
    nfrm, px, py, chunks, per, frames, parts = dims
    nplane = px * py
    trk, me = lax.axis_index("trk"), lax.axis_index("frm")
    spot, half = lax.div(trk, 2), lax.rem(trk, 2)
    x, y = lax.div(spot, py), lax.rem(spot, py)
    width = HEADS * HEAD
    few = frames // parts
    owned = chunks * per
    keys = nfrm * frames
    tracks, virtuals = y1.shape[1], vq.shape[1]
    unit_rows = few * virtuals // nplane
    batch = owned // 2
    group = min(4, few)

    def column(k):
        return lax.rem(me + k, nfrm)

    def along_x(i):
        return lax.rem(x + i, px)

    def along_y(i):
        return lax.rem(y + i, py)

    def place(xx, yy):
        return ((xx * py + yy) * 2 + half, me)

    def in_plane(i):
        other = lax.rem(spot + i, nplane)
        return (other * 2 + half, me)

    def remote(src, dst, sems, where):
        return pltpu.make_async_remote_copy(
            src_ref=src,
            dst_ref=dst,
            send_sem=sems[0],
            recv_sem=sems[1],
            device_id=where,
            device_id_type=MESH,
        )

    def each(count, act):
        def body(k, carry):
            act(k)
            return carry

        lax.fori_loop(1, count, body, 0)

    weights = (w_time_qkv, w_time_o, w_read_q, w_read_kv, w_read_o, w_write_q, w_write_kv, w_write_o)
    offsets = []
    at = 0
    loads = []
    for n, w in enumerate(weights):
        cols = w.shape[1]
        offsets.append((at, cols))
        loads.append(pltpu.make_async_copy(w, raw.at[:, pl.ds(at, cols)], load_sem.at[n]))
        at += cols
    for w, dst in ((w_up, r_up), (w_down, r_down), (v_up, r_vup), (v_down, r_vdown), (virtual, virt), (tokens, tok)):
        loads.append(pltpu.make_async_copy(w, dst, load_sem.at[len(loads)]))
    own = pltpu.make_async_copy(tokens.at[me], x_recv.at[me], own_sem)

    barrier = pltpu.get_barrier_semaphore()
    partner = (trk + 1 - 2 * half, me)
    pl.semaphore_signal(barrier, inc=1, device_id=partner, device_id_type=MESH)
    each(
        nfrm,
        lambda k: pl.semaphore_signal(barrier, inc=1, device_id=(trk, column(k)), device_id_type=MESH),
    )
    each(
        nplane,
        lambda i: pl.semaphore_signal(barrier, inc=1, device_id=in_plane(i), device_id_type=MESH),
    )
    pl.semaphore_wait(barrier, nfrm - 1 + nplane - 1 + 1)

    def vis_rows(p):
        return pl.ds(pl.multiple_of(p * owned, owned), owned)

    def vis_copy(k):
        return remote(
            vis.at[vis_rows(column(k))],
            vis_recv.at[me],
            (vis_sem.at[0, k], vis_sem.at[1, k]),
            (trk, column(k)),
        )

    def tok_copy(c, k):
        return remote(
            tokens.at[column(k), pl.ds(c * per, per)],
            x_recv.at[me, pl.ds(c * per, per)],
            (tok_sem.at[0, c, k], tok_sem.at[1, c, k]),
            (trk, column(k)),
        )

    def back_copy(n, k):
        return remote(
            stage.at[n, column(k)],
            y_recv.at[n, me],
            (back_sem.at[0, n, k], back_sem.at[1, n, k]),
            (trk, column(k)),
        )

    each(nfrm, lambda k: vis_copy(k).start())
    for c in range(chunks):
        each(nfrm, lambda k: tok_copy(c, k).start())
    own.start()
    for load in loads:
        load.start()

    for load in loads:
        load.wait()
    cols_to = spread_matrix(False)
    rows_to = spread_matrix(True)

    def pad_cols(n, dst):
        start, cols = offsets[n]
        for b in range(cols // width):
            block = raw[:, start + b * width : start + (b + 1) * width]
            dst[:, b * WIDE : (b + 1) * WIDE] = dot(block, cols_to).astype(bf16)

    def pad_rows(n, dst):
        start, cols = offsets[n]
        dst[...] = dot(rows_to, raw[:, start : start + cols]).astype(bf16)

    pad_cols(0, p_time_qkv)
    pad_rows(1, p_time_o)
    pad_cols(2, p_read_q)
    pad_cols(3, p_read_kv)
    pad_rows(4, p_read_o)
    pad_cols(5, p_write_q)
    pad_cols(6, p_write_kv)
    pad_rows(7, p_write_o)

    for h in range(parts):
        rows = virt[h].reshape(few * virtuals, width).astype(f32)
        normed = (unit(rows) * gains[4:5, :]).astype(bf16)
        queries = dot(normed, p_read_q[...]).astype(bf16)
        vq[h * few : (h + 1) * few] = queries.reshape(few, virtuals, WIDE)

    flipped = jnp.transpose((vis[...].astype(f32) - 1.0) * PENALTY)
    read_bias[...] = jnp.concatenate([flipped, flipped], axis=-1)

    each(nfrm, lambda k: vis_copy(k).wait_recv())
    vis_recv[pl.ds(me, 1)] = vis[vis_rows(me)][None]
    row_bias = jnp.concatenate(
        [vis_recv[s][:, h * few : (h + 1) * few] for h in range(parts) for s in range(nfrm)], axis=-1
    )
    time_bias[...] = (row_bias.astype(f32) - 1.0) * PENALTY
    own.wait()

    def project(c, carry):
        each(nfrm, lambda k: tok_copy(c, k).wait_recv())
        rows = []
        for t in range(per):
            blocks = [x_recv[s, c * per + t].astype(f32) for s in range(nfrm)]
            rows += [b[h * few : (h + 1) * few] for h in range(parts) for b in blocks]
        rows = jnp.concatenate(rows, axis=0)
        normed = (unit(rows) * gains[0:1, :]).astype(bf16)
        triple = dot(normed, p_time_qkv[...]).astype(bf16)
        qkv[pl.ds(c * per, per)] = triple.reshape(per, keys, 3 * WIDE)
        return carry

    lax.fori_loop(0, chunks, project, 0)
    asked = keys // parts

    def attend(n, carry):
        h, first = lax.div(n, 2), lax.rem(n, 2) * batch
        lane_k, lane_q = lanes(keys), lanes(asked)
        blocks = [(t, p) for t in range(batch) for p in range(PAIRS)]
        bias = [time_bias[pl.ds(first + t, 1), :] for t in range(batch)]
        bias = [jnp.concatenate([b, b], axis=-1) for b in bias]

        def piece(m, t, p):
            cols = slice(m * WIDE + p * TILE, m * WIDE + (p + 1) * TILE)
            if m == 0:
                return qkv[first + t, pl.ds(pl.multiple_of(h * asked, asked), asked), cols]
            return qkv[first + t, :, cols]

        scores = [dot_t(piece(0, t, p), halves(piece(1, t, p), lane_k)) * SCALE + bias[t] for t, p in blocks]
        heads = [s[:, m * keys : (m + 1) * keys] for s in scores for m in range(2)]
        peaks = [jnp.max(s, axis=-1, keepdims=True) for s in heads]
        expos = [jnp.exp(s - m) for s, m in zip(heads, peaks)]
        dens = [jnp.sum(e, axis=-1, keepdims=True) for e in expos]
        expos = [e.astype(bf16) for e in expos]
        nums = [
            dot(jnp.concatenate(expos[2 * m : 2 * m + 2], axis=-1), halves(piece(2, t, p), lane_k))
            for m, (t, p) in enumerate(blocks)
        ]
        tiles = [
            (num / jnp.where(lane_q < SLOT, dens[2 * m], dens[2 * m + 1])).astype(bf16)
            for m, num in enumerate(nums)
        ]
        outs = [jnp.concatenate(tiles[t * PAIRS : (t + 1) * PAIRS], axis=-1) for t in range(batch)]
        projected = dot(jnp.concatenate(outs, axis=0), p_time_o[...])
        for s in range(nfrm):
            mine = [
                projected[t * asked + s * few : t * asked + (s + 1) * few] for t in range(batch)
            ]
            stage[n, s] = jnp.concatenate(mine, axis=0).astype(bf16)
        each(nfrm, lambda k: back_copy(n, k).start())
        y_recv[pl.ds(n, 1), pl.ds(me, 1)] = stage[pl.ds(n, 1), pl.ds(me, 1)]
        return carry

    lax.fori_loop(0, 2 * parts, attend, 0)

    def add(h):
        for b in range(2):
            n = h * 2 + b
            each(nfrm, lambda k: back_copy(n, k).wait_recv())
            for o in range(nfrm):
                old = tok[o, b * batch : (b + 1) * batch].astype(f32)[:, h * few : (h + 1) * few]
                total = old + y_recv[n, o].astype(f32).reshape(batch, few, width)
                total = total.astype(bf16).astype(f32).reshape(batch * few, width)
                start = (o * owned + b * batch) * few
                for m in range(width // TILE):
                    y1t[m, start : start + batch * few, :] = total[:, m * TILE : (m + 1) * TILE]
        rows = []
        for f in range(few):
            rows.append(
                jnp.concatenate(
                    [y1t[m, pl.ds(f, tracks, stride=few), :] for m in range(width // TILE)], axis=-1
                )
            )
        rows = jnp.concatenate(rows, axis=0)
        span = slice(h * few, (h + 1) * few)
        y1[span] = rows.astype(bf16).reshape(few, tracks, width)
        normed = (unit(rows) * gains[1:2, :]).astype(bf16)
        kv2[span] = dot(normed, p_read_kv[...]).astype(bf16).reshape(few, tracks, 2 * WIDE)

    def write_queries(h):
        span = slice(h * few, (h + 1) * few)
        rows = y1[span].reshape(few * tracks, width).astype(f32)
        normed = (unit(rows) * gains[2:3, :]).astype(bf16)
        wq[span] = dot(normed, p_write_q[...]).astype(bf16).reshape(few, tracks, WIDE)

    low, high = pl.ds(0, WIDE // 2), pl.ds(WIDE // 2, WIDE // 2)

    def one_x_copy(h, i):
        return remote(
            pay.at[h, along_x(i), :, :, low],
            one_x.at[h, x],
            (part_sem.at[0, h, 0, i], part_sem.at[1, h, 0, i]),
            place(along_x(i), y),
        )

    def one_y_copy(h, i):
        return remote(
            pay.at[h, :, along_y(i), :, high],
            one_y.at[h, y],
            (part_sem.at[0, h, 1, i], part_sem.at[1, h, 1, i]),
            place(x, along_y(i)),
        )

    def two_y_copy(h, i):
        return remote(
            mid_x.at[h, along_y(i)],
            two_y.at[h, y],
            (part_sem.at[0, h, 2, i], part_sem.at[1, h, 2, i]),
            place(x, along_y(i)),
        )

    def two_x_copy(h, i):
        return remote(
            mid_y.at[h, along_x(i)],
            two_x.at[h, x],
            (part_sem.at[0, h, 3, i], part_sem.at[1, h, 3, i]),
            place(along_x(i), y),
        )

    def across(h):
        return remote(
            cross.at[h, half], cross.at[h, half], (cross_sem.at[0, h], cross_sem.at[1, h]), partner
        )

    def gather_copy(h, i):
        return remote(
            vout.at[h, x, y],
            vout.at[h, x, y],
            (gather_sem.at[0, h, i], gather_sem.at[1, h, i]),
            in_plane(i),
        )

    def read(h):
        at = [p * TILE for p in range(PAIRS)]
        for g in range(few // group):
            inside = [h * few + g * group + n for n in range(group)]
            nums, peaks = pair_attention(
                [vq[f, :, a : a + TILE] for f in inside for a in at],
                [kv2[f, :, a : a + TILE] for f in inside for a in at],
                [kv2[f, :, WIDE + a : WIDE + a + TILE] for f in inside for a in at],
                [read_bias[f : f + 1, :] for f in inside for a in at],
            )
            tiles = [with_peak(num, peak) for num, peak in zip(nums, peaks)]
            for n in range(group):
                rows = jnp.concatenate(tiles[n * PAIRS : (n + 1) * PAIRS], axis=-1)
                for r in range(0, virtuals, unit_rows):
                    u = ((g * group + n) * virtuals + r) // unit_rows
                    pay[h, u // py, u % py] = rows[r : r + unit_rows]
        each(px, lambda i: one_x_copy(h, i).start())
        each(py, lambda i: one_y_copy(h, i).start())
        one_x[pl.ds(h, 1), pl.ds(x, 1)] = pay[pl.ds(h, 1), pl.ds(x, 1), :, :, : WIDE // 2]
        one_y[h, pl.ds(y, 1)] = pay[h, :, pl.ds(y, 1), :, WIDE // 2 :].reshape(1, px, unit_rows, WIDE // 2)

    def middle_step(h):
        each(px, lambda i: one_x_copy(h, i).wait_recv())
        merged = merge_tiles(one_x[h].reshape(px, py * unit_rows, WIDE // 2))
        mid_x[h] = merged.reshape(py, unit_rows, WIDE // 2)
        each(py, lambda i: two_y_copy(h, i).start())
        two_y[h, pl.ds(y, 1)] = mid_x[h, pl.ds(y, 1)]
        each(py, lambda i: one_y_copy(h, i).wait_recv())
        merged = merge_tiles(one_y[h].reshape(py, px * unit_rows, WIDE // 2))
        mid_y[h] = merged.reshape(px, unit_rows, WIDE // 2)
        each(px, lambda i: two_x_copy(h, i).start())
        two_x[h, pl.ds(x, 1)] = mid_y[h, pl.ds(x, 1)]

    def cross_step(h):
        each(py, lambda i: two_y_copy(h, i).wait_recv())
        lower = merge_tiles(two_y[h])
        each(px, lambda i: two_x_copy(h, i).wait_recv())
        upper = merge_tiles(two_x[h])
        cross[h, pl.ds(half, 1)] = jnp.concatenate([lower, upper], axis=-1)[None]
        across(h).start()

    def virtual_step(h):
        across(h).wait_recv()
        both = cross[h]
        readout = jnp.concatenate(
            [over_den(merge(both[:, :, p * TILE : (p + 1) * TILE])[0]) for p in range(PAIRS)], axis=-1
        )
        virt1 = (virt[h, x, y].astype(f32) + dot(readout, p_read_o[...])).astype(bf16).astype(f32)
        normed = (unit(virt1) * gains[5:6, :]).astype(bf16)
        middle = gelu(dot(normed, r_vup[...])).astype(bf16)
        vout[h, x, y] = (virt1 + dot(middle, r_vdown[...])).astype(bf16)
        each(nplane, lambda i: gather_copy(h, i).start())

    def out_copy(h, g):
        span = pl.ds(h * few + g * group, group)
        return pltpu.make_async_copy(outv.at[span], track_out.at[span], out_sem.at[h * (few // group) + g])

    def write(h, g):
        if g == 0:
            each(nplane, lambda i: gather_copy(h, i).wait_recv())
        count = group * virtuals // unit_rows
        units = [g * count + n for n in range(count)]
        rows = jnp.concatenate([vout[h, u // py, u % py] for u in units], axis=0).astype(f32)
        normed = (unit(rows) * gains[6:7, :]).astype(bf16)
        pairs = dot(normed, p_write_kv[...]).astype(bf16)
        span = slice(h * few + g * group, h * few + (g + 1) * group)
        at = [p * TILE for p in range(PAIRS)]
        blocks = [pairs[n * virtuals : (n + 1) * virtuals] for n in range(group)]
        nums, _ = pair_attention(
            [wq[f, :, a : a + TILE] for f in range(span.start, span.stop) for a in at],
            [block[:, a : a + TILE] for block in blocks for a in at],
            [block[:, WIDE + a : WIDE + a + TILE] for block in blocks for a in at],
            None,
        )
        tiles = [over_den(num) for num in nums]
        outs = [jnp.concatenate(tiles[n * PAIRS : (n + 1) * PAIRS], axis=-1) for n in range(group)]
        first = y1[span].reshape(group * tracks, width).astype(f32)
        second = first + dot(jnp.concatenate(outs, axis=0), p_write_o[...])
        second = second.astype(bf16).astype(f32)
        normed = (unit(second) * gains[3:4, :]).astype(bf16)
        middle = gelu(dot(normed, r_up[...])).astype(bf16)
        final = second + dot(middle, r_down[...])
        outv[span] = final.astype(bf16).reshape(group, tracks, width)
        out_copy(h, g).start()

    add(0)
    read(0)
    write_queries(0)
    middle_step(0)
    cross_step(0)
    add(1)
    read(1)
    virtual_step(0)
    write_queries(1)
    middle_step(1)
    cross_step(1)
    write(0, 0)
    virtual_step(1)
    for g in range(1, few // group):
        write(0, g)
    for g in range(few // group):
        write(1, g)

    virt_done = pltpu.make_async_copy(vout, virt_out, own_sem)
    virt_done.start()

    each(nfrm, lambda k: vis_copy(k).wait_send())
    for c in range(chunks):
        each(nfrm, lambda k: tok_copy(c, k).wait_send())
    for n in range(2 * parts):
        each(nfrm, lambda k: back_copy(n, k).wait_send())
    for h in range(parts):
        each(px, lambda i: one_x_copy(h, i).wait_send())
        each(py, lambda i: one_y_copy(h, i).wait_send())
        each(py, lambda i: two_y_copy(h, i).wait_send())
        each(px, lambda i: two_x_copy(h, i).wait_send())
        across(h).wait_send()
        each(nplane, lambda i: gather_copy(h, i).wait_send())
        for g in range(few // group):
            out_copy(h, g).wait()
    virt_done.wait()


def shards(tokens, visible, virtual, gains, *weights):
    tracks, frames, width = tokens.shape
    nfrm, nplane = lax.axis_size("frm"), lax.axis_size("trk") // 2
    virtuals = virtual.shape[1]
    py = math.isqrt(nplane)
    px = nplane // py
    owned = tracks // nfrm
    chunks, parts = 4, 2
    per = owned // chunks
    few = frames // parts
    unit_rows = few * virtuals // nplane
    hidden = weights[8].shape[1]
    keys = nfrm * frames
    dims = (nfrm, px, py, chunks, per, frames, parts)
    narrow = (nfrm, owned, frames, width)
    shares = (parts, px, py, unit_rows, width)
    vmem, anywhere = pl.BlockSpec(memory_space=pltpu.VMEM), pl.BlockSpec(memory_space=pl.ANY)
    dma = pltpu.SemaphoreType.DMA
    raw_cols = sum(w.shape[1] for w in weights[:8])
    track_out, virt_out = pl.pallas_call(
        functools.partial(kernel, dims),
        out_shape=(
            jax.ShapeDtypeStruct((frames, tracks, width), bf16),
            jax.ShapeDtypeStruct(shares, bf16),
        ),
        in_specs=[anywhere, vmem, anywhere, vmem] + [anywhere] * 12,
        out_specs=(anywhere, anywhere),
        scratch_shapes=[
            pltpu.VMEM(narrow, bf16),
            pltpu.VMEM(narrow, bf16),
            pltpu.VMEM((owned, keys, 3 * WIDE), bf16),
            pltpu.VMEM((2 * parts, nfrm, owned // 2 * few, width), bf16),
            pltpu.VMEM((2 * parts, nfrm, owned // 2 * few, width), bf16),
            pltpu.VMEM((nfrm, owned, frames), jnp.int32),
            pltpu.VMEM((owned, keys), f32),
            pltpu.VMEM((frames, 2 * tracks), f32),
            pltpu.VMEM((width // TILE, tracks * few, TILE), f32),
            pltpu.VMEM((frames, tracks, width), bf16),
            pltpu.VMEM(shares, bf16),
            pltpu.VMEM((frames, virtuals, WIDE), bf16),
            pltpu.VMEM((frames, tracks, 2 * WIDE), bf16),
            pltpu.VMEM((frames, tracks, WIDE), bf16),
            pltpu.VMEM((parts, px, py, unit_rows, WIDE), bf16),
            pltpu.VMEM((parts, px, py, unit_rows, WIDE // 2), bf16),
            pltpu.VMEM((parts, py, px, unit_rows, WIDE // 2), bf16),
            pltpu.VMEM((parts, py, unit_rows, WIDE // 2), bf16),
            pltpu.VMEM((parts, px, unit_rows, WIDE // 2), bf16),
            pltpu.VMEM((parts, px, unit_rows, WIDE // 2), bf16),
            pltpu.VMEM((parts, py, unit_rows, WIDE // 2), bf16),
            pltpu.VMEM((parts, 2, unit_rows, WIDE), bf16),
            pltpu.VMEM(shares, bf16),
            pltpu.VMEM((frames, tracks, width), bf16),
            pltpu.VMEM((width, raw_cols), bf16),
            pltpu.VMEM((width, hidden), bf16),
            pltpu.VMEM((hidden, width), bf16),
            pltpu.VMEM((width, hidden), bf16),
            pltpu.VMEM((hidden, width), bf16),
            pltpu.VMEM((width, 3 * WIDE), bf16),
            pltpu.VMEM((WIDE, width), bf16),
            pltpu.VMEM((width, WIDE), bf16),
            pltpu.VMEM((width, 2 * WIDE), bf16),
            pltpu.VMEM((WIDE, width), bf16),
            pltpu.VMEM((width, WIDE), bf16),
            pltpu.VMEM((width, 2 * WIDE), bf16),
            pltpu.VMEM((WIDE, width), bf16),
            dma((14,)),
            dma,
            dma((2, nfrm)),
            dma((2, chunks, nfrm)),
            dma((2, 2 * parts, nfrm)),
            dma((2, parts, 4, max(px, py))),
            dma((2, parts)),
            dma((2, parts, nplane)),
            dma((frames,)),
        ],
        compiler_params=pltpu.CompilerParams(
            collective_id=0, has_side_effects=True, vmem_limit_bytes=56 * 1024 * 1024
        ),
    )(tokens.reshape(narrow), visible, virtual.reshape(shares), gains, *weights)
    return jnp.transpose(track_out, (1, 0, 2)), virt_out.reshape(frames, virtuals, width)


def solution(mesh):
    in_specs = (P("trk", "frm", None), P("trk", "frm"), P("frm", None, None)) + (P(),) * 13
    out_specs = (P("trk", "frm", None), P("frm", None, None))
    return jax.shard_map(shards, mesh=mesh, in_specs=in_specs, out_specs=out_specs, check_vma=False)
```

time: 125 us -> 95.8 us (0.77)
  the two profiles are of different devices: /device:TPU:8 before, /device:TPU:32 now
where the time goes in v2:
time: 95.8 us; the launch traced here: 95.6 us
  Pallas kernels  90.2 us (94%)
  local copies, waits for them, and re-layouts  4.82 us (5%)
    pallas_call x1, Pallas kernels, shards(): pl.pallas_call(functools.partial(kernel, dims), out_shape=(jax.ShapeDtype...  90.2 us
    unnamed x5, local copies, waits for them, and re-layouts  4.82 us

profile of v2, /device:TPU:32, one launch (start us, length us, event | category | flops | bytes accessed | tf_op | source)
XLA Modules:
  0.0 95.6 jit_solution(7690697433405110752)
XLA Ops:
  0.6 1.4 %copy.18.vis = s32[64,16]{1,0:T(8,128)} copy(s32[64,16]{0,1:T(8,128)} %param.17) | data formatting | bytes 8192 | tf_op args[1]
  2.0 90.2 %shard_map.167 = (bf16[16,64,384]{2,1,0:T(8,128)(2,1)}, bf16[2,4,4,32,384]{4,3,2,1,0:T(8,128)(2,1)}) custom-call(bf16[8,8,16,384]{3,2,1,0:T(8,128)(2,1)} %bitcast.6, s32[64,16]{1,0:T(8,128)} %copy.18.vis, bf16[2,4,4,32,384]{4,3,2,1,0:T(8,128)(2,1)} %bitcast.7, f32[7,384]{1,0:T(8,128)} %gains.1, bf16[384,1152]{1,0:T(8,128)(2,1)} %w_time_qkv.1, ...), custom_call_target="tpu_custom_call" | custom-call | tf_op jit(solution)/shard_map/pallas_call | solution.py:615
  92.2 0.0 copy-start
  92.2 2.5 %copy.19 = bf16[64,16,384]{2,1,0:T(8,128)(2,1)} copy(bf16[64,16,384]{2,0,1:T(8,128)(2,1)} %bitcast.5) | data formatting | bytes 1572864
  94.7 0.0 copy-done
  94.7 0.9 copy.21
Async XLA Ops:
  92.2 2.6 %copy-start = (bf16[2,4,4,32,384]{4,3,2,1,0:T(8,128)(2,1)S(1)}, bf16[2,4,4,32,384]{4,3,2,1,0:T(8,128)(2,1)}, u32[]{:S(2)}) copy-start(bf16[2,4,4,32,384]{4,3,2,1,0:T(8,128)(2,1)} %get-tuple-element.5) | copy-start | bytes 2359300

commit v3 on v2

--- a/solution.py
+++ b/solution.py
@@ -66,10 +66,16 @@
     return jnp.where(lane < SLOT, lane, lane - SLOT)
 
 
+def sum_columns(keys):
+    row = lax.broadcasted_iota(jnp.int32, (2 * keys, TILE), 0)
+    col = lax.broadcasted_iota(jnp.int32, (2 * keys, TILE), 1)
+    return jnp.where((row < keys) == (col < SLOT), 1.0, 0.0).astype(bf16)
+
+
 def pair_attention(qs, ks, vs, biases):
-    lane_k, lane_q = lanes(ks[0].shape[0]), lanes(qs[0].shape[0])
-    marked = slot_lanes(ks[0].shape[0]) == HEAD
-    vs = [jnp.where(marked, jnp.ones_like(v), v) for v in vs]
+    keys = ks[0].shape[0]
+    lane_k, lane_q = lanes(keys), lanes(qs[0].shape[0])
+    ones = sum_columns(keys)
     scores = [dot_t(q, halves(k, lane_k)) * SCALE for q, k in zip(qs, ks)]
     if biases is not None:
         scores = [s + b for s, b in zip(scores, biases)]
@@ -78,7 +84,8 @@
     second = [jnp.max(jnp.where(left, -jnp.inf, s), axis=-1, keepdims=True) for s in scores]
     peaks = [jnp.where(left, x, y) for x, y in zip(first, second)]
     expos = [jnp.exp(s - p).astype(bf16) for s, p in zip(scores, peaks)]
-    return [dot(e, halves(v, lane_k)) for e, v in zip(expos, vs)], peaks
+    sums = [dot(e, jnp.concatenate([halves(v, lane_k), ones], axis=-1)) for e, v in zip(expos, vs)]
+    return [x[:, :TILE] for x in sums], [x[:, TILE:] for x in sums], peaks
 
 
 def with_peak(num, peak):
@@ -91,6 +98,10 @@
     num = jnp.where(place == HEAD + 2, mid, num)
     num = jnp.where(place == HEAD + 3, low, num)
     return num.astype(bf16)
+
+
+def with_den(num, den):
+    return jnp.where(slot_lanes(num.shape[0]) == HEAD, den, num)
 
 
 def over_den(num):
@@ -126,7 +137,7 @@
 def kernel(
     dims,
     tokens,
-    vis,
+    visible,
     virtual,
     gains,
     w_time_qkv,
@@ -148,6 +159,7 @@
     qkv,
     stage,
     y_recv,
+    vis,
     vis_recv,
     time_bias,
     read_bias,
@@ -158,12 +170,7 @@
     kv2,
     wq,
     pay,
-    one_x,
-    one_y,
-    mid_x,
-    mid_y,
-    two_x,
-    two_y,
+    part,
     cross,
     vout,
     outv,
@@ -190,11 +197,9 @@
     gather_sem,
     out_sem,
 ):
-    nfrm, px, py, chunks, per, frames, parts = dims
-    nplane = px * py
+    nfrm, nplane, chunks, per, frames, parts = dims
     trk, me = lax.axis_index("trk"), lax.axis_index("frm")
     spot, half = lax.div(trk, 2), lax.rem(trk, 2)
-    x, y = lax.div(spot, py), lax.rem(spot, py)
     width = HEADS * HEAD
     few = frames // parts
     owned = chunks * per
@@ -202,23 +207,9 @@
     tracks, virtuals = y1.shape[1], vq.shape[1]
     unit_rows = few * virtuals // nplane
     batch = owned // 2
-    group = min(4, few)
 
     def column(k):
         return lax.rem(me + k, nfrm)
-
-    def along_x(i):
-        return lax.rem(x + i, px)
-
-    def along_y(i):
-        return lax.rem(y + i, py)
-
-    def place(xx, yy):
-        return ((xx * py + yy) * 2 + half, me)
-
-    def in_plane(i):
-        other = lax.rem(spot + i, nplane)
-        return (other * 2 + half, me)
 
     def remote(src, dst, sems, where):
         return pltpu.make_async_remote_copy(
@@ -248,6 +239,7 @@
         at += cols
     for w, dst in ((w_up, r_up), (w_down, r_down), (v_up, r_vup), (v_down, r_vdown), (virtual, virt), (tokens, tok)):
         loads.append(pltpu.make_async_copy(w, dst, load_sem.at[len(loads)]))
+    loads.append(pltpu.make_async_copy(visible, vis, load_sem.at[len(loads)]))
     own = pltpu.make_async_copy(tokens.at[me], x_recv.at[me], own_sem)
 
     barrier = pltpu.get_barrier_semaphore()
@@ -259,19 +251,15 @@
     )
     each(
         nplane,
-        lambda i: pl.semaphore_signal(barrier, inc=1, device_id=in_plane(i), device_id_type=MESH),
+        lambda i: pl.semaphore_signal(
+            barrier, inc=1, device_id=(lax.rem(spot + i, nplane) * 2 + half, me), device_id_type=MESH
+        ),
     )
     pl.semaphore_wait(barrier, nfrm - 1 + nplane - 1 + 1)
 
-    def vis_rows(p):
-        return pl.ds(pl.multiple_of(p * owned, owned), owned)
-
     def vis_copy(k):
         return remote(
-            vis.at[vis_rows(column(k))],
-            vis_recv.at[me],
-            (vis_sem.at[0, k], vis_sem.at[1, k]),
-            (trk, column(k)),
+            visible, vis_recv.at[me], (vis_sem.at[0, k], vis_sem.at[1, k]), (trk, column(k))
         )
 
     def tok_copy(c, k):
@@ -327,15 +315,17 @@
         queries = dot(normed, p_read_q[...]).astype(bf16)
         vq[h * few : (h + 1) * few] = queries.reshape(few, virtuals, WIDE)
 
-    flipped = jnp.transpose((vis[...].astype(f32) - 1.0) * PENALTY)
+    flipped = (vis[...].astype(f32) - 1.0) * PENALTY
     read_bias[...] = jnp.concatenate([flipped, flipped], axis=-1)
 
     each(nfrm, lambda k: vis_copy(k).wait_recv())
-    vis_recv[pl.ds(me, 1)] = vis[vis_rows(me)][None]
-    row_bias = jnp.concatenate(
-        [vis_recv[s][:, h * few : (h + 1) * few] for h in range(parts) for s in range(nfrm)], axis=-1
-    )
-    time_bias[...] = (row_bias.astype(f32) - 1.0) * PENALTY
+    vis_recv[pl.ds(me, 1)] = vis[...][None]
+    seen = [vis_recv[s].astype(f32) for s in range(nfrm)]
+    seen = [s[h * few : (h + 1) * few] for h in range(parts) for s in seen]
+    row = lax.broadcasted_iota(jnp.int32, (owned, tracks), 0)
+    col = lax.broadcasted_iota(jnp.int32, (owned, tracks), 1)
+    pick = jnp.where(col == row + me * owned, 1.0, 0.0).astype(bf16)
+    time_bias[...] = (dot_t(pick, jnp.concatenate(seen, axis=0).astype(bf16)) - 1.0) * PENALTY
     own.wait()
 
     def project(c, carry):
@@ -353,33 +343,32 @@
     lax.fori_loop(0, chunks, project, 0)
     asked = keys // parts
 
-    def attend(n, carry):
-        h, first = lax.div(n, 2), lax.rem(n, 2) * batch
-        lane_k, lane_q = lanes(keys), lanes(asked)
+    def attend(n):
+        h, first = n // 2, n % 2 * batch
+        lane_k = lanes(keys)
         blocks = [(t, p) for t in range(batch) for p in range(PAIRS)]
-        bias = [time_bias[pl.ds(first + t, 1), :] for t in range(batch)]
+        bias = [time_bias[first + t : first + t + 1, :] for t in range(batch)]
         bias = [jnp.concatenate([b, b], axis=-1) for b in bias]
 
         def piece(m, t, p):
             cols = slice(m * WIDE + p * TILE, m * WIDE + (p + 1) * TILE)
             if m == 0:
-                return qkv[first + t, pl.ds(pl.multiple_of(h * asked, asked), asked), cols]
+                return qkv[first + t, h * asked : (h + 1) * asked, cols]
             return qkv[first + t, :, cols]
 
         scores = [dot_t(piece(0, t, p), halves(piece(1, t, p), lane_k)) * SCALE + bias[t] for t, p in blocks]
         heads = [s[:, m * keys : (m + 1) * keys] for s in scores for m in range(2)]
         peaks = [jnp.max(s, axis=-1, keepdims=True) for s in heads]
-        expos = [jnp.exp(s - m) for s, m in zip(heads, peaks)]
-        dens = [jnp.sum(e, axis=-1, keepdims=True) for e in expos]
-        expos = [e.astype(bf16) for e in expos]
-        nums = [
-            dot(jnp.concatenate(expos[2 * m : 2 * m + 2], axis=-1), halves(piece(2, t, p), lane_k))
+        expos = [jnp.exp(s - m).astype(bf16) for s, m in zip(heads, peaks)]
+        ones = sum_columns(keys)
+        sums = [
+            dot(
+                jnp.concatenate(expos[2 * m : 2 * m + 2], axis=-1),
+                jnp.concatenate([halves(piece(2, t, p), lane_k), ones], axis=-1),
+            )
             for m, (t, p) in enumerate(blocks)
         ]
-        tiles = [
-            (num / jnp.where(lane_q < SLOT, dens[2 * m], dens[2 * m + 1])).astype(bf16)
-            for m, num in enumerate(nums)
-        ]
+        tiles = [(x[:, :TILE] / x[:, TILE:]).astype(bf16) for x in sums]
         outs = [jnp.concatenate(tiles[t * PAIRS : (t + 1) * PAIRS], axis=-1) for t in range(batch)]
         projected = dot(jnp.concatenate(outs, axis=0), p_time_o[...])
         for s in range(nfrm):
@@ -387,11 +376,19 @@
                 projected[t * asked + s * few : t * asked + (s + 1) * few] for t in range(batch)
             ]
             stage[n, s] = jnp.concatenate(mine, axis=0).astype(bf16)
+        if n < 2:
+            each(nfrm, lambda k: back_copy(n, k).start())
+        y_recv[n, pl.ds(me, 1)] = stage[n, pl.ds(me, 1)]
+
+    for n in range(2 * parts):
+        attend(n)
+
+    def send_back(n):
         each(nfrm, lambda k: back_copy(n, k).start())
-        y_recv[pl.ds(n, 1), pl.ds(me, 1)] = stage[pl.ds(n, 1), pl.ds(me, 1)]
-        return carry
-
-    lax.fori_loop(0, 2 * parts, attend, 0)
+
+    each(nfrm, lambda k: back_copy(0, k).wait_send())
+    each(nfrm, lambda k: back_copy(1, k).wait_send())
+    send_back(2)
 
     def add(h):
         for b in range(2):
@@ -423,38 +420,13 @@
         normed = (unit(rows) * gains[2:3, :]).astype(bf16)
         wq[span] = dot(normed, p_write_q[...]).astype(bf16).reshape(few, tracks, WIDE)
 
-    low, high = pl.ds(0, WIDE // 2), pl.ds(WIDE // 2, WIDE // 2)
-
-    def one_x_copy(h, i):
+    def part_copy(h, i):
+        other = lax.rem(spot + i, nplane)
         return remote(
-            pay.at[h, along_x(i), :, :, low],
-            one_x.at[h, x],
-            (part_sem.at[0, h, 0, i], part_sem.at[1, h, 0, i]),
-            place(along_x(i), y),
-        )
-
-    def one_y_copy(h, i):
-        return remote(
-            pay.at[h, :, along_y(i), :, high],
-            one_y.at[h, y],
-            (part_sem.at[0, h, 1, i], part_sem.at[1, h, 1, i]),
-            place(x, along_y(i)),
-        )
-
-    def two_y_copy(h, i):
-        return remote(
-            mid_x.at[h, along_y(i)],
-            two_y.at[h, y],
-            (part_sem.at[0, h, 2, i], part_sem.at[1, h, 2, i]),
-            place(x, along_y(i)),
-        )
-
-    def two_x_copy(h, i):
-        return remote(
-            mid_y.at[h, along_x(i)],
-            two_x.at[h, x],
-            (part_sem.at[0, h, 3, i], part_sem.at[1, h, 3, i]),
-            place(along_x(i), y),
+            pay.at[h, other],
+            part.at[h, spot],
+            (part_sem.at[0, h, i], part_sem.at[1, h, i]),
+            (other * 2 + half, me),
         )
 
     def across(h):
@@ -464,51 +436,33 @@
 
     def gather_copy(h, i):
         return remote(
-            vout.at[h, x, y],
-            vout.at[h, x, y],
+            vout.at[h, spot],
+            vout.at[h, spot],
             (gather_sem.at[0, h, i], gather_sem.at[1, h, i]),
-            in_plane(i),
+            (lax.rem(spot + i, nplane) * 2 + half, me),
         )
 
     def read(h):
         at = [p * TILE for p in range(PAIRS)]
-        for g in range(few // group):
-            inside = [h * few + g * group + n for n in range(group)]
-            nums, peaks = pair_attention(
-                [vq[f, :, a : a + TILE] for f in inside for a in at],
-                [kv2[f, :, a : a + TILE] for f in inside for a in at],
-                [kv2[f, :, WIDE + a : WIDE + a + TILE] for f in inside for a in at],
-                [read_bias[f : f + 1, :] for f in inside for a in at],
-            )
-            tiles = [with_peak(num, peak) for num, peak in zip(nums, peaks)]
-            for n in range(group):
-                rows = jnp.concatenate(tiles[n * PAIRS : (n + 1) * PAIRS], axis=-1)
-                for r in range(0, virtuals, unit_rows):
-                    u = ((g * group + n) * virtuals + r) // unit_rows
-                    pay[h, u // py, u % py] = rows[r : r + unit_rows]
-        each(px, lambda i: one_x_copy(h, i).start())
-        each(py, lambda i: one_y_copy(h, i).start())
-        one_x[pl.ds(h, 1), pl.ds(x, 1)] = pay[pl.ds(h, 1), pl.ds(x, 1), :, :, : WIDE // 2]
-        one_y[h, pl.ds(y, 1)] = pay[h, :, pl.ds(y, 1), :, WIDE // 2 :].reshape(1, px, unit_rows, WIDE // 2)
-
-    def middle_step(h):
-        each(px, lambda i: one_x_copy(h, i).wait_recv())
-        merged = merge_tiles(one_x[h].reshape(px, py * unit_rows, WIDE // 2))
-        mid_x[h] = merged.reshape(py, unit_rows, WIDE // 2)
-        each(py, lambda i: two_y_copy(h, i).start())
-        two_y[h, pl.ds(y, 1)] = mid_x[h, pl.ds(y, 1)]
-        each(py, lambda i: one_y_copy(h, i).wait_recv())
-        merged = merge_tiles(one_y[h].reshape(py, px * unit_rows, WIDE // 2))
-        mid_y[h] = merged.reshape(px, unit_rows, WIDE // 2)
-        each(px, lambda i: two_x_copy(h, i).start())
-        two_x[h, pl.ds(x, 1)] = mid_y[h, pl.ds(x, 1)]
+        inside = range(h * few, (h + 1) * few)
+        nums, dens, peaks = pair_attention(
+            [vq[f, :, a : a + TILE] for f in inside for a in at],
+            [kv2[f, :, a : a + TILE] for f in inside for a in at],
+            [kv2[f, :, WIDE + a : WIDE + a + TILE] for f in inside for a in at],
+            [read_bias[f : f + 1, :] for f in inside for a in at],
+        )
+        tiles = [with_peak(with_den(num, den), peak) for num, den, peak in zip(nums, dens, peaks)]
+        for n in range(few):
+            rows = jnp.concatenate(tiles[n * PAIRS : (n + 1) * PAIRS], axis=-1)
+            for r in range(0, virtuals, unit_rows):
+                u = (n * virtuals + r) // unit_rows
+                pay[h, u] = rows[r : r + unit_rows]
+        each(nplane, lambda i: part_copy(h, i).start())
+        part[h, pl.ds(spot, 1)] = pay[h, pl.ds(spot, 1)]
 
     def cross_step(h):
-        each(py, lambda i: two_y_copy(h, i).wait_recv())
-        lower = merge_tiles(two_y[h])
-        each(px, lambda i: two_x_copy(h, i).wait_recv())
-        upper = merge_tiles(two_x[h])
-        cross[h, pl.ds(half, 1)] = jnp.concatenate([lower, upper], axis=-1)[None]
+        each(nplane, lambda i: part_copy(h, i).wait_recv())
+        cross[h, pl.ds(half, 1)] = merge_tiles(part[h])[None]
         across(h).start()
 
     def virtual_step(h):
@@ -517,34 +471,33 @@
         readout = jnp.concatenate(
             [over_den(merge(both[:, :, p * TILE : (p + 1) * TILE])[0]) for p in range(PAIRS)], axis=-1
         )
-        virt1 = (virt[h, x, y].astype(f32) + dot(readout, p_read_o[...])).astype(bf16).astype(f32)
+        virt1 = (virt[h, spot].astype(f32) + dot(readout, p_read_o[...])).astype(bf16).astype(f32)
         normed = (unit(virt1) * gains[5:6, :]).astype(bf16)
         middle = gelu(dot(normed, r_vup[...])).astype(bf16)
-        vout[h, x, y] = (virt1 + dot(middle, r_vdown[...])).astype(bf16)
+        vout[h, spot] = (virt1 + dot(middle, r_vdown[...])).astype(bf16)
         each(nplane, lambda i: gather_copy(h, i).start())
 
-    def out_copy(h, g):
-        span = pl.ds(h * few + g * group, group)
-        return pltpu.make_async_copy(outv.at[span], track_out.at[span], out_sem.at[h * (few // group) + g])
-
-    def write(h, g):
+    def out_copy(at, group):
+        span = pl.ds(at, group)
+        return pltpu.make_async_copy(outv.at[span], track_out.at[span], out_sem.at[at])
+
+    def write(h, g, group):
         if g == 0:
             each(nplane, lambda i: gather_copy(h, i).wait_recv())
-        count = group * virtuals // unit_rows
-        units = [g * count + n for n in range(count)]
-        rows = jnp.concatenate([vout[h, u // py, u % py] for u in units], axis=0).astype(f32)
+        units = range(g * virtuals // unit_rows, (g + group) * virtuals // unit_rows)
+        rows = jnp.concatenate([vout[h, u] for u in units], axis=0).astype(f32)
         normed = (unit(rows) * gains[6:7, :]).astype(bf16)
         pairs = dot(normed, p_write_kv[...]).astype(bf16)
-        span = slice(h * few + g * group, h * few + (g + 1) * group)
+        span = slice(h * few + g, h * few + g + group)
         at = [p * TILE for p in range(PAIRS)]
         blocks = [pairs[n * virtuals : (n + 1) * virtuals] for n in range(group)]
-        nums, _ = pair_attention(
+        nums, dens, _ = pair_attention(
             [wq[f, :, a : a + TILE] for f in range(span.start, span.stop) for a in at],
             [block[:, a : a + TILE] for block in blocks for a in at],
             [block[:, WIDE + a : WIDE + a + TILE] for block in blocks for a in at],
             None,
         )
-        tiles = [over_den(num) for num in nums]
+        tiles = [(num / den).astype(bf16) for num, den in zip(nums, dens)]
         outs = [jnp.concatenate(tiles[n * PAIRS : (n + 1) * PAIRS], axis=-1) for n in range(group)]
         first = y1[span].reshape(group * tracks, width).astype(f32)
         second = first + dot(jnp.concatenate(outs, axis=0), p_write_o[...])
@@ -553,25 +506,24 @@
         middle = gelu(dot(normed, r_up[...])).astype(bf16)
         final = second + dot(middle, r_down[...])
         outv[span] = final.astype(bf16).reshape(group, tracks, width)
-        out_copy(h, g).start()
-
+        out_copy(span.start, group).start()
+
+    some = few // 2
+    written = ((0, some), (some, few - some), (few, few))
     add(0)
     read(0)
+    send_back(3)
     write_queries(0)
-    middle_step(0)
     cross_step(0)
     add(1)
     read(1)
     virtual_step(0)
     write_queries(1)
-    middle_step(1)
     cross_step(1)
-    write(0, 0)
+    write(0, 0, some)
     virtual_step(1)
-    for g in range(1, few // group):
-        write(0, g)
-    for g in range(few // group):
-        write(1, g)
+    write(0, some, few - some)
+    write(1, 0, few)
 
     virt_done = pltpu.make_async_copy(vout, virt_out, own_sem)
     virt_done.start()
@@ -579,17 +531,14 @@
     each(nfrm, lambda k: vis_copy(k).wait_send())
     for c in range(chunks):
         each(nfrm, lambda k: tok_copy(c, k).wait_send())
-    for n in range(2 * parts):
+    for n in range(2 * parts - 2, 2 * parts):
         each(nfrm, lambda k: back_copy(n, k).wait_send())
     for h in range(parts):
-        each(px, lambda i: one_x_copy(h, i).wait_send())
-        each(py, lambda i: one_y_copy(h, i).wait_send())
-        each(py, lambda i: two_y_copy(h, i).wait_send())
-        each(px, lambda i: two_x_copy(h, i).wait_send())
+        each(nplane, lambda i: part_copy(h, i).wait_send())
         across(h).wait_send()
         each(nplane, lambda i: gather_copy(h, i).wait_send())
-        for g in range(few // group):
-            out_copy(h, g).wait()
+    for start, count in written:
+        out_copy(start, count).wait()
     virt_done.wait()
 
 
@@ -597,18 +546,16 @@
     tracks, frames, width = tokens.shape
     nfrm, nplane = lax.axis_size("frm"), lax.axis_size("trk") // 2
     virtuals = virtual.shape[1]
-    py = math.isqrt(nplane)
-    px = nplane // py
     owned = tracks // nfrm
-    chunks, parts = 4, 2
+    chunks, parts = 2, 2
     per = owned // chunks
     few = frames // parts
     unit_rows = few * virtuals // nplane
     hidden = weights[8].shape[1]
     keys = nfrm * frames
-    dims = (nfrm, px, py, chunks, per, frames, parts)
+    dims = (nfrm, nplane, chunks, per, frames, parts)
     narrow = (nfrm, owned, frames, width)
-    shares = (parts, px, py, unit_rows, width)
+    shares = (parts, nplane, unit_rows, width)
     vmem, anywhere = pl.BlockSpec(memory_space=pltpu.VMEM), pl.BlockSpec(memory_space=pl.ANY)
     dma = pltpu.SemaphoreType.DMA
     raw_cols = sum(w.shape[1] for w in weights[:8])
@@ -618,7 +565,7 @@
             jax.ShapeDtypeStruct((frames, tracks, width), bf16),
             jax.ShapeDtypeStruct(shares, bf16),
         ),
-        in_specs=[anywhere, vmem, anywhere, vmem] + [anywhere] * 12,
+        in_specs=[anywhere, anywhere, anywhere, vmem] + [anywhere] * 12,
         out_specs=(anywhere, anywhere),
         scratch_shapes=[
             pltpu.VMEM(narrow, bf16),
@@ -626,7 +573,8 @@
             pltpu.VMEM((owned, keys, 3 * WIDE), bf16),
             pltpu.VMEM((2 * parts, nfrm, owned // 2 * few, width), bf16),
             pltpu.VMEM((2 * parts, nfrm, owned // 2 * few, width), bf16),
-            pltpu.VMEM((nfrm, owned, frames), jnp.int32),
+            pltpu.VMEM((frames, tracks), jnp.int32),
+            pltpu.VMEM((nfrm, frames, tracks), jnp.int32),
             pltpu.VMEM((owned, keys), f32),
             pltpu.VMEM((frames, 2 * tracks), f32),
             pltpu.VMEM((width // TILE, tracks * few, TILE), f32),
@@ -635,13 +583,8 @@
             pltpu.VMEM((frames, virtuals, WIDE), bf16),
             pltpu.VMEM((frames, tracks, 2 * WIDE), bf16),
             pltpu.VMEM((frames, tracks, WIDE), bf16),
-            pltpu.VMEM((parts, px, py, unit_rows, WIDE), bf16),
-            pltpu.VMEM((parts, px, py, unit_rows, WIDE // 2), bf16),
-            pltpu.VMEM((parts, py, px, unit_rows, WIDE // 2), bf16),
-            pltpu.VMEM((parts, py, unit_rows, WIDE // 2), bf16),
-            pltpu.VMEM((parts, px, unit_rows, WIDE // 2), bf16),
-            pltpu.VMEM((parts, px, unit_rows, WIDE // 2), bf16),
-            pltpu.VMEM((parts, py, unit_rows, WIDE // 2), bf16),
+            pltpu.VMEM((parts, nplane, unit_rows, WIDE), bf16),
+            pltpu.VMEM((parts, nplane, unit_rows, WIDE), bf16),
             pltpu.VMEM((parts, 2, unit_rows, WIDE), bf16),
             pltpu.VMEM(shares, bf16),
             pltpu.VMEM((frames, tracks, width), bf16),
@@ -658,12 +601,12 @@
             pltpu.VMEM((width, WIDE), bf16),
             pltpu.VMEM((width, 2 * WIDE), bf16),
             pltpu.VMEM((WIDE, width), bf16),
-            dma((14,)),
+            dma((15,)),
             dma,
             dma((2, nfrm)),
             dma((2, chunks, nfrm)),
             dma((2, 2 * parts, nfrm)),
-            dma((2, parts, 4, max(px, py))),
+            dma((2, parts, nplane)),
             dma((2, parts)),
             dma((2, parts, nplane)),
             dma((frames,)),
@@ -671,7 +614,7 @@
         compiler_params=pltpu.CompilerParams(
             collective_id=0, has_side_effects=True, vmem_limit_bytes=56 * 1024 * 1024
         ),
-    )(tokens.reshape(narrow), visible, virtual.reshape(shares), gains, *weights)
+    )(tokens.reshape(narrow), jnp.transpose(visible), virtual.reshape(shares), gains, *weights)
     return jnp.transpose(track_out, (1, 0, 2)), virt_out.reshape(frames, virtuals, width)
 
 

time: 95.8 us -> 92.1 us (0.961)
  Pallas kernels: 90.2 us -> 87 us
  local copies, waits for them, and re-layouts: 4.82 us -> 3.43 us
    pallas_call x1, Pallas kernels: 90.2 us -> 87 us  [shards(): pl.pallas_call(functools.partial(kernel, dims), out_shape=(jax.ShapeDtype...]
    unnamed x5 -> x4, local copies, waits for them, and re-layouts: 4.82 us -> 3.43 us
where the time goes in v3:
time: 92.1 us; the launch traced here: 91.1 us
  Pallas kernels  87 us (94%)
  local copies, waits for them, and re-layouts  3.43 us (4%)
    pallas_call x1, Pallas kernels, shards(): pl.pallas_call(functools.partial(kernel, dims), out_shape=(jax.ShapeDtype...  87 us
    unnamed x4, local copies, waits for them, and re-layouts  3.43 us

profile of v3, /device:TPU:32, one launch (start us, length us, event | category | flops | bytes accessed | tf_op | source)
XLA Modules:
  0.0 91.1 jit_solution(6497646352262662721)
XLA Ops:
  0.6 87.0 %shard_map.167 = (bf16[16,64,384]{2,1,0:T(8,128)(2,1)}, bf16[2,16,32,384]{3,2,1,0:T(8,128)(2,1)}) custom-call(bf16[8,8,16,384]{3,2,1,0:T(8,128)(2,1)} %bitcast.5, s32[16,64]{1,0:T(8,128)} %bitcast.9, bf16[2,16,32,384]{3,2,1,0:T(8,128)(2,1)} %bitcast.6, f32[7,384]{1,0:T(8,128)} %gains.1, bf16[384,1152]{1,0:T(8,128)(2,1)} %w_time_qkv.1, ...), custom_call_target="tpu_custom_call" | custom-call | tf_op jit(solution)/shard_map/pallas_call | solution.py:562
  87.6 0.0 copy-start
  87.6 2.5 %copy.18 = bf16[64,16,384]{2,1,0:T(8,128)(2,1)} copy(bf16[64,16,384]{2,0,1:T(8,128)(2,1)} %bitcast.8) | data formatting | bytes 1572864
  90.2 0.0 copy-done
  90.2 0.9 copy.20
Async XLA Ops:
  87.6 2.6 %copy-start = (bf16[2,16,32,384]{3,2,1,0:T(8,128)(2,1)S(1)}, bf16[2,16,32,384]{3,2,1,0:T(8,128)(2,1)}, u32[]{:S(2)}) copy-start(bf16[2,16,32,384]{3,2,1,0:T(8,128)(2,1)} %get-tuple-element.5) | copy-start | bytes 2359300

commit v4 on v3

--- a/solution.py
+++ b/solution.py
@@ -386,9 +386,13 @@
     def send_back(n):
         each(nfrm, lambda k: back_copy(n, k).start())
 
-    each(nfrm, lambda k: back_copy(0, k).wait_send())
-    each(nfrm, lambda k: back_copy(1, k).wait_send())
-    send_back(2)
+    def next_part(h):
+        for n in (2 * h - 2, 2 * h - 1):
+            each(nfrm, lambda k: back_copy(n, k).wait_send())
+        send_back(2 * h)
+        send_back(2 * h + 1)
+
+    next_part(1)
 
     def add(h):
         for b in range(2):
@@ -508,22 +512,33 @@
         outv[span] = final.astype(bf16).reshape(group, tracks, width)
         out_copy(span.start, group).start()
 
-    some = few // 2
-    written = ((0, some), (some, few - some), (few, few))
+    written = [(h * few, few) for h in range(parts)]
     add(0)
     read(0)
-    send_back(3)
+    next_part(2)
     write_queries(0)
-    cross_step(0)
     add(1)
     read(1)
+    next_part(3)
+    cross_step(0)
+    write_queries(1)
+    add(2)
+    read(2)
+    cross_step(1)
     virtual_step(0)
-    write_queries(1)
-    cross_step(1)
-    write(0, 0, some)
+    write_queries(2)
+    add(3)
+    read(3)
+    cross_step(2)
     virtual_step(1)
-    write(0, some, few - some)
+    write_queries(3)
+    write(0, 0, few)
+    cross_step(3)
+    virtual_step(2)
     write(1, 0, few)
+    virtual_step(3)
+    write(2, 0, few)
+    write(3, 0, few)
 
     virt_done = pltpu.make_async_copy(vout, virt_out, own_sem)
     virt_done.start()
@@ -547,7 +562,7 @@
     nfrm, nplane = lax.axis_size("frm"), lax.axis_size("trk") // 2
     virtuals = virtual.shape[1]
     owned = tracks // nfrm
-    chunks, parts = 2, 2
+    chunks, parts = 2, 4
     per = owned // chunks
     few = frames // parts
     unit_rows = few * virtuals // nplane

time: 92.1 us -> 86.7 us (0.941)
  Pallas kernels: 87 us -> 81.9 us
    pallas_call x1, Pallas kernels: 87 us -> 81.9 us  [shards(): pl.pallas_call(functools.partial(kernel, dims), out_shape=(jax.ShapeDtype...]
where the time goes in v4:
time: 86.7 us; the launch traced here: 86 us
  Pallas kernels  81.9 us (94%)
  local copies, waits for them, and re-layouts  3.43 us (4%)
    pallas_call x1, Pallas kernels, shards(): pl.pallas_call(functools.partial(kernel, dims), out_shape=(jax.ShapeDtype...  81.9 us
    unnamed x4, local copies, waits for them, and re-layouts  3.43 us

profile of v4, /device:TPU:32, one launch (start us, length us, event | category | flops | bytes accessed | tf_op | source)
XLA Modules:
  0.0 86.0 jit_solution(13603276413285763590)
XLA Ops:
  0.6 81.9 %shard_map.167 = (bf16[16,64,384]{2,1,0:T(8,128)(2,1)}, bf16[4,16,16,384]{3,2,1,0:T(8,128)(2,1)}) custom-call(bf16[8,8,16,384]{3,2,1,0:T(8,128)(2,1)} %bitcast.5, s32[16,64]{1,0:T(8,128)} %bitcast.9, bf16[4,16,16,384]{3,2,1,0:T(8,128)(2,1)} %bitcast.6, f32[7,384]{1,0:T(8,128)} %gains.1, bf16[384,1152]{1,0:T(8,128)(2,1)} %w_time_qkv.1, ...), custom_call_target="tpu_custom_call" | custom-call | tf_op jit(solution)/shard_map/pallas_call | solution.py:577
  82.6 0.0 copy-start
  82.6 2.5 %copy.18 = bf16[64,16,384]{2,1,0:T(8,128)(2,1)} copy(bf16[64,16,384]{2,0,1:T(8,128)(2,1)} %bitcast.8) | data formatting | bytes 1572864
  85.1 0.0 copy-done
  85.1 0.9 %copy.20 = bf16[16,64,384]{2,1,0:T(8,128)(2,1)} copy(bf16[16,64,384]{2,1,0:T(8,128)(2,1)S(1)} %bitcast.7) | data formatting | bytes 1572864
Async XLA Ops:
  82.6 2.6 %copy-start = (bf16[4,16,16,384]{3,2,1,0:T(8,128)(2,1)S(1)}, bf16[4,16,16,384]{3,2,1,0:T(8,128)(2,1)}, u32[]{:S(2)}) copy-start(bf16[4,16,16,384]{3,2,1,0:T(8,128)(2,1)} %get-tuple-element.5) | copy-start | bytes 2359300

commit v5 on v4

--- a/solution.py
+++ b/solution.py
@@ -519,8 +519,8 @@
     write_queries(0)
     add(1)
     read(1)
+    cross_step(0)
     next_part(3)
-    cross_step(0)
     write_queries(1)
     add(2)
     read(2)

time: 86.7 us -> 86 us (level)
  no operation moved by 1% of the time
where the time goes in v5:
time: 86 us; the launch traced here: 85.7 us
  Pallas kernels  81.6 us (95%)
  local copies, waits for them, and re-layouts  3.43 us (4%)
    pallas_call x1, Pallas kernels, shards(): pl.pallas_call(functools.partial(kernel, dims), out_shape=(jax.ShapeDtype...  81.6 us
    unnamed x4, local copies, waits for them, and re-layouts  3.43 us

profile of v5, /device:TPU:32, one launch (start us, length us, event | category | flops | bytes accessed | tf_op | source)
XLA Modules:
  0.0 85.7 jit_solution(11695578418310246827)
XLA Ops:
  0.6 81.6 %shard_map.167 = (bf16[16,64,384]{2,1,0:T(8,128)(2,1)}, bf16[4,16,16,384]{3,2,1,0:T(8,128)(2,1)}) custom-call(bf16[8,8,16,384]{3,2,1,0:T(8,128)(2,1)} %bitcast.5, s32[16,64]{1,0:T(8,128)} %bitcast.9, bf16[4,16,16,384]{3,2,1,0:T(8,128)(2,1)} %bitcast.6, f32[7,384]{1,0:T(8,128)} %gains.1, bf16[384,1152]{1,0:T(8,128)(2,1)} %w_time_qkv.1, ...), custom_call_target="tpu_custom_call" | custom-call | tf_op jit(solution)/shard_map/pallas_call | solution.py:577
  82.3 0.0 copy-start
  82.3 2.5 %copy.18 = bf16[64,16,384]{2,1,0:T(8,128)(2,1)} copy(bf16[64,16,384]{2,0,1:T(8,128)(2,1)} %bitcast.8) | data formatting | bytes 1572864
  84.8 0.0 copy-done
  84.8 0.9 %copy.20 = bf16[16,64,384]{2,1,0:T(8,128)(2,1)} copy(bf16[16,64,384]{2,1,0:T(8,128)(2,1)S(1)} %bitcast.7) | data formatting | bytes 1572864
Async XLA Ops:
  82.3 2.6 %copy-start = (bf16[4,16,16,384]{3,2,1,0:T(8,128)(2,1)S(1)}, bf16[4,16,16,384]{3,2,1,0:T(8,128)(2,1)}, u32[]{:S(2)}) copy-start(bf16[4,16,16,384]{3,2,1,0:T(8,128)(2,1)} %get-tuple-element.5) | copy-start | bytes 2359300
